TPU v7x, 512 devices: a whole 4x4x16 slice. The times are simulated.
512 devices in a mesh: tok: 16 (over y, x), col: 32 (over z, core).
Axes of the slice: x: 4, y: 4, z: 16, core: 2. Of those that a mesh axis runs over, the one named last changes fastest.
Arguments:
- rollout: bfloat16 [2048, 5120], P('tok'), may hold values from -6 to 6
- lengths: int32 [32], P('tok'), may hold values from 16 to 64
- route: int32 [2048, 1], P('tok'), may hold values from 0 to 15; in each aligned block of 128 rows (0 to 127, 128 to 255, ...) at most 16 rows name the same one
- up_codes: bfloat16 [5120, 16384], P('tok', 'col'), may hold values from -4 to 4
- up_scales: float32 [20, 64], P(None, 'col'), may hold values from 0.0069877123 to 0.02795085
- block_rows: int32 [64, 2], P('col'), may hold values from 0 to 19, as said below
- delta: float32 [256, 64, 2, 256], P('tok', 'col'), may hold values from -0.125 to 0.125
- adam_m: float32 [256, 64, 2, 256], P('tok', 'col'), may hold values from -12 to 12
- adam_v: float32 [256, 64, 2, 256], P('tok', 'col'), may hold values from 1 to 30
- gate_pre: bfloat16 [4096, 16384], P('tok', 'col'), may hold values from -8 to 8
- hidden_grad: bfloat16 [4096, 16384], P('tok', 'col'), may hold values from -0.875 to 0.875
Outputs:
- input_grad: bfloat16 [4096, 5120], P('tok', 'col')
- gate_grad: bfloat16 [4096, 16384], P('tok', 'col')
- new_delta: float32 [256, 64, 2, 256], P('tok', 'col')
- new_m: float32 [256, 64, 2, 256], P('tok', 'col')
- new_v: float32 [256, 64, 2, 256], P('tok', 'col')
- delta_scale: float32 [64, 2], P('col')
- delta_codes: bfloat16 [256, 64, 2, 256], P('tok', 'col')
Inputs may be any that keep to these rules, and one draw needn't show every extreme that they name: `route`: at most 16 of the 128 rows of one index of tok name the same learner shard, and some learner shard is named by exactly 16 of them. `block_rows`: the 2 row blocks of one column block are distinct.
All inputs are finite; a program needn't handle non-finite values. Where the computation divides by a largest or mean magnitude, that divisor is 1e-20 or more.
Results may differ from a plain program's by a relative error of at most 0.017.
Values may be sent and summed in bfloat16 or wider, within the bound.
A program may use at most 128 MiB of HBM per device.

v0:
```python
import jax
import jax.numpy as jnp
from jax import lax
from jax.sharding import PartitionSpec as P

BLK = 256
K = 2
RESP = 64
STEP = 1000


beta_first = 0.9
beta_second = 0.999
step_rate = 0.01
adam_eps = 1e-08
scale_eps = 1e-06


def silu_slope(operand):
    sigmoid_value = jax.nn.sigmoid(operand)
    return sigmoid_value * (1.0 + operand * (1.0 - sigmoid_value))


def dequant(code_rows, scales):
    row_count = code_rows.shape[0]
    block_count = scales.shape[0]
    width_blocks = scales.shape[1]
    block_of_row = jnp.arange(row_count, dtype=jnp.int32) // BLK
    selector = (block_of_row[:, None] == jnp.arange(block_count, dtype=jnp.int32)[None, :]).astype(
        jnp.float32
    )
    row_scales = jnp.dot(selector, scales, precision=lax.Precision.HIGHEST)
    spread = (
        code_rows.astype(jnp.float32).reshape(row_count, width_blocks, -1) * row_scales[:, :, None]
    )
    return spread.reshape(row_count, -1).astype(jnp.bfloat16)


def per_device(
    rollout,
    lengths,
    route,
    up_codes,
    up_scales,
    block_rows,
    delta,
    adam_m,
    adam_v,
    gate_pre,
    hidden_grad,
):
    peer_count = lax.axis_size("tok")
    send_rows = rollout.shape[0]
    row_width = rollout.shape[1]
    capacity = 2 * send_rows // peer_count
    row_ids = jnp.arange(send_rows, dtype=jnp.int32)
    seq_len = jnp.repeat(lengths, RESP)
    position = row_ids % RESP
    row_weight = jnp.where(position < seq_len, RESP / seq_len.astype(jnp.float32), 0.0)
    destination = route[:, 0]
    onehot = (destination[:, None] == jnp.arange(peer_count, dtype=jnp.int32)[None, :]).astype(
        jnp.int32
    )
    slot_index = jnp.sum((jnp.cumsum(onehot, axis=0) - 1) * onehot, axis=1)
    target = destination * capacity + slot_index
    weight_slots = (
        jnp.zeros((peer_count * capacity,), jnp.float32)
        .at[target]
        .set(row_weight)
        .reshape(peer_count, capacity)
    )
    buffer = (
        jnp.zeros((peer_count * capacity, row_width), jnp.bfloat16)
        .at[target]
        .set(rollout)
        .reshape(peer_count, capacity, row_width)
    )
    arrived, arrived_weight = (
        lax.all_to_all(buffer, "tok", split_axis=0, concat_axis=0, tiled=True),
        lax.all_to_all(
            weight_slots.astype(jnp.bfloat16), "tok", split_axis=0, concat_axis=0, tiled=True
        ).astype(weight_slots.dtype),
    )
    learn_x = arrived.reshape(peer_count * capacity, row_width)
    learn_w = arrived_weight.reshape(peer_count * capacity)
    rows_learn = learn_x.shape[0]
    column_count = up_codes.shape[1]
    blocks_here = column_count // BLK
    block_total = up_scales.shape[0]
    delta_full = lax.all_gather(delta.astype(jnp.bfloat16), "tok", axis=0, tiled=True)
    chosen = jnp.take(
        learn_x.reshape(rows_learn, block_total, BLK), block_rows.reshape(-1), axis=1
    ).reshape(rows_learn, blocks_here, K, BLK)
    activation = jax.nn.silu(gate_pre.astype(jnp.float32))
    up_grad = (hidden_grad.astype(jnp.float32) * activation * learn_w[:, None]).astype(jnp.bfloat16)
    up_grad_blocks = up_grad.reshape(rows_learn, blocks_here, BLK)
    delta_up = jnp.einsum(
        "rjkb,bjkc->rjc", chosen, delta_full, preferred_element_type=jnp.float32
    ).reshape(rows_learn, column_count)
    delta_back = jnp.einsum(
        "rjc,bjkc->rjkb", up_grad_blocks, delta_full, preferred_element_type=jnp.float32
    )
    selector = (
        block_rows.reshape(-1)[:, None] == jnp.arange(block_total, dtype=jnp.int32)[None, :]
    ).astype(jnp.float32)
    delta_input = jnp.einsum(
        "rqb,qd->rdb",
        delta_back.reshape(rows_learn, -1, BLK),
        selector,
        precision=lax.Precision.HIGHEST,
    ).reshape(rows_learn, row_width)
    weight = dequant(lax.all_gather(up_codes, "tok", axis=0, tiled=True), up_scales)
    base_up = jnp.dot(learn_x, weight, preferred_element_type=jnp.float32)
    weight = dequant(lax.all_gather(up_codes, "tok", axis=0, tiled=True), up_scales)
    base_input = lax.dot_general(
        up_grad, weight, (((1,), (1,)), ((), ())), preferred_element_type=jnp.float32
    )
    up_value = base_up + delta_up
    gate_grad = (
        hidden_grad.astype(jnp.float32)
        * up_value
        * silu_slope(gate_pre.astype(jnp.float32))
        * learn_w[:, None]
    ).astype(jnp.bfloat16)
    input_grad = lax.psum_scatter(
        base_input + delta_input, "col", scatter_dimension=1, tiled=True
    ).astype(jnp.bfloat16)
    owned_rows = BLK // peer_count
    summed_grad = lax.psum(
        jnp.einsum("rjkb,rjc->bjkc", chosen, up_grad_blocks, preferred_element_type=jnp.float32),
        "tok",
    )
    gradient = lax.dynamic_slice_in_dim(
        summed_grad, lax.axis_index("tok") * owned_rows, owned_rows, 0
    )
    new_m = beta_first * adam_m + (1.0 - beta_first) * gradient
    new_v = beta_second * adam_v + (1.0 - beta_second) * gradient * gradient
    corrected_m = new_m / (1.0 - beta_first**STEP)
    corrected_v = new_v / (1.0 - beta_second**STEP)
    new_delta = delta - step_rate * corrected_m / (jnp.sqrt(corrected_v) + adam_eps)
    local_max = jnp.max(jnp.abs(new_delta), axis=(0, 3))
    block_scale = lax.pmax(local_max, "tok")
    new_codes = (new_delta / (block_scale + scale_eps)[None, :, :, None]).astype(jnp.bfloat16)
    return (input_grad, gate_grad, new_delta, new_m, new_v, block_scale, new_codes)


def solution(mesh):
    placed = (
        P("tok", None),
        P("tok"),
        P("tok", None),
        P("tok", "col"),
        P(None, "col"),
        P("col", None),
        P("tok", "col", None, None),
        P("tok", "col", None, None),
        P("tok", "col", None, None),
        P("tok", "col"),
        P("tok", "col"),
    )
    return jax.shard_map(
        per_device,
        mesh=mesh,
        in_specs=placed,
        out_specs=(
            P("tok", "col"),
            P("tok", "col"),
            P("tok", "col", None, None),
            P("tok", "col", None, None),
            P("tok", "col", None, None),
            P("col", None),
            P("tok", "col", None, None),
        ),
        check_vma=False,
    )
```

profile of v0, /device:TPU:1, one launch (start us, length us, event | category | flops | bytes accessed | tf_op | source)
XLA Modules:
  0.0 365.2 jit_solution(11603398601671209707)
XLA Ops:
  7.2 0.0 copy-start
  7.2 0.0 copy-start.4
  7.2 0.0 copy-start.2
  7.2 0.0 all-gather.2.cloned.1.call-start
  7.2 0.7 all-gather.2.cloned.1.call-update
  7.9 0.7 broadcast_in_dim.21
  8.7 0.1 reshape.118
  8.7 0.7 fusion.23
  9.5 0.2 reduce_window_sum.11
  9.7 0.8 select_reduce_fusion
  10.5 0.7 fusion.30
  11.2 1.0 scatter_custom_fusion
  12.2 0.7 convert_element_type.79
  12.9 7.6 %all-to-all-start = ((bf16[16,1,16]{2,1,0:T(2,128)(2,1)}), bf16[16,1,16]{2,1,0:T(2,128)(2,1)S(1)}, u32[]{:S(2)}, u32[]{:S(2)}) async-start(bf16[16,1,16]{2,1,0:T(2,128)(2,1)} %convert_element_type.79), calls=%async_computation | async-start | bytes 16384 | tf_op jit(solution)/shard_map/all_to_all | solution.py:80
  20.4 5.0 %scatter_custom_fusion.1 = bf16[256,5120]{1,0:T(8,128)(2,1)} fusion(s32[128]{0:T(128)S(1)} %fusion.30, bf16[128,5120]{1,0:T(8,128)(2,1)} %param.11, bf16[]{:T(256)} %constant.85.clone.1), kind=kCustom, calls=%fused_computation.7 | custom fusion | bytes 2621952 | tf_op jit(solution)/shard_map/scatter | solution.py:75
  25.5 1.3 all-to-all-done
  26.8 5.4 %all-to-all-start.1 = ((bf16[16,16,5120]{2,1,0:T(8,128)(2,1)}), bf16[16,16,5120]{2,1,0:T(8,128)(2,1)S(1)}, u32[]{:S(2)}, u32[]{:S(2)}) async-start(bf16[16,16,5120]{2,1,0:T(8,128)(2,1)} %bitcast.47), calls=%async_computation.2 | async-start | bytes 5242880 | tf_op jit(solution)/shard_map/all_to_all | solution.py:79
  32.1 0.0 all-reduce.2.cloned.1.call-start
  32.2 0.0 copy-done.4
  32.2 0.1 eq.59
  32.3 0.1 reshape.124
  32.4 0.0 copy-done.2
  32.4 0.0 copy-done
  32.4 1.5 fusion.18
  33.9 6.1 %mul.101 = f32[5120,2,256]{2,1,0:T(2,128)S(1)} broadcast(f32[5120,2]{1,0:T(8,128)S(1)} %fusion.18), dimensions={0,1} | broadcast | bytes 10526720 | tf_op jit(solution)/shard_map/mul | solution.py:34
  40.0 5.2 %copy.114 = f32[640,8,2,256]{3,1,2,0:T(8,128)} copy(f32[640,8,2,256]{3,2,1,0:T(2,128)S(1)} %bitcast.44) | data formatting | bytes 20971520
  45.3 38.5 %all_gather.8 = bf16[256,2,2,256]{3,0,2,1:T(8,128)(2,1)S(1)} all-gather(bf16[16,2,2,256]{3,0,2,1:T(8,128)(2,1)S(1)} %copy.125), channel_id=1, replica_groups=mesh['tok'=16,'col'=32] {'tok'}, dimensions={0}, use_global_device_ids=true | all-gather | bytes 557056 | tf_op jit(solution)/shard_map/all_gather | solution.py:90
  83.8 0.1 reshape.126
  83.9 1.2 fusion.8
  85.1 0.8 reshape.119
  85.9 1.8 copy.107
  87.7 1.3 fusion.38
  89.0 4.9 %convolution_bitcast_fusion = f32[256,20,256]{2,1,0:T(8,128)} fusion(f32[256,4,256]{2,0,1:T(8,128)S(1)} %bitcast.50, s32[4]{0:T(128)S(1)} %eq.59), kind=kOutput, calls=%fused_computation.5 | convolution fusion | flops 62914640 | bytes 6291472 | tf_op jit(solution)/shard_map/rqb,qd->rdb/dot_general | solution.py:106
  93.9 6.4 %copy.92 = f32[256,20,256]{0,2,1:T(8,128)} copy(f32[256,20,256]{2,1,0:T(8,128)} %convolution_bitcast_fusion) | data formatting | bytes 10485760 | tf_op jit(solution)/shard_map/rqb,qd->rdb/transpose | solution.py:106
  100.3 0.0 all-to-all-done.1
  100.3 3.0 reshape_reshape.3
  103.4 4.0 %copy.93 = bf16[256,20,256]{2,0,1:T(8,128)(2,1)} copy(bf16[256,20,256]{2,1,0:T(8,128)(2,1)} %reshape_reshape.3) | data formatting | bytes 5242880 | tf_op jit(solution)/shard_map/reshape;reshape | solution.py:92
  107.4 3.1 gather_fusion
  110.5 2.5 convolution_bitcast_fusion.1
  113.0 0.0 all-reduce.2.cloned.1.call-update
  113.1 0.0 reduce-scatter.2.cloned.1.call-start
  113.1 0.0 all-gather.2.cloned.1.call-done
  113.1 11.0 %convolution_add_fusion = f32[256,5120]{0,1:T(8,128)} fusion(f32[256,5120]{0,1:T(8,128)} %bitcast.46, bf16[256,512]{1,0:T(8,128)(2,1)S(1)} %fusion.8, f32[5120,512]{1,0:T(8,128)} %bitcast.42, bf16[5120,512]{1,0:T(8,128)(2,1)} %all-gather.2.cloned.1.call-done), kind=kOutput, calls=%fused_computation.4 | convolution fusion | flops 1351352320 | bytes 26476544 | tf_op jit(solution)/shard_map/dot_general | solution.py:115
  124.1 0.0 copy-start.1
  124.1 0.0 reduce-scatter.2.cloned.1.call-update
  124.2 2.3 fusion.15
  126.5 1.2 copy.111
  127.7 112.9 %all-reduce.2.cloned.1.call-done = f32[256,2,2,256]{3,0,2,1:T(8,128)} async-done(((f32[256,2,2,256]{3,0,2,1:T(8,128)}), f32[256,2,2,256]{3,0,2,1:T(8,128)}) %all-reduce.2.cloned.1.call-update) | async-done | bytes 1048592 | tf_op jit(solution)/shard_map/psum | solution.py:129
  240.7 1.6 abs_reduce_fusion
  242.3 30.9 %pmax.7 = f32[2,2]{1,0:T(2,128)S(1)} all-reduce(f32[2,2]{1,0:T(2,128)S(1)} %get-tuple-element.42), channel_id=1, replica_groups=mesh['tok'=16,'col'=32] {'tok'}, use_global_device_ids=true, to_apply=%region_7.8 | all-reduce | flops 4 | bytes 32 | tf_op jit(solution)/shard_map/pmax | solution.py:142
  273.1 0.0 copy-start.3
  273.1 0.7 copy.100
  273.8 1.5 copy.101
  275.4 1.5 copy.102
  276.9 0.1 divide_convert_fusion
  277.0 0.6 copy.103
  277.6 0.0 copy-done.1
  277.6 8.2 %fusion.5 = bf16[256,512]{1,0:T(8,128)(2,1)} fusion(f32[256,512]{1,0:T(8,128)S(1)} %copy.111, bf16[256,5120]{1,0:T(8,128)(2,1)S(1)} %bitcast.45, bf16[256,512]{1,0:T(8,128)(2,1)S(1)} %copy-done.1, bf16[256,512]{1,0:T(8,128)(2,1)} %param.20, f32[256]{0:T(256)S(1)} %reshape.126, f32[5120,512]{1,0:T(8,128)} %bitcast.43, ...), kind=kOutput, calls=%fused_computation.13 | convolution fusion | flops 1351876608 | bytes 19661824 | tf_op jit(solution)/shard_map/dot_general | solution.py:113
  285.8 0.0 copy-done.3
  285.8 71.3 %reduce-scatter.2.cloned.1.call-done = f32[256,160]{0,1:T(8,128)} async-done(((f32[256,5120]{0,1:T(8,128)}), f32[256,160]{0,1:T(8,128)}) %reduce-scatter.2.cloned.1.call-update) | async-done | bytes 163856 | tf_op jit(solution)/shard_map/reduce_scatter | solution.py:125
  357.1 1.6 convert_element_type.75
  (9 shorter events, 0.1 us)
Async XLA Ops:
  7.2 25.2 %copy-start = (f32[20,2]{0,1:T(2,128)S(1)}, f32[20,2]{0,1:T(2,128)}, u32[]{:S(2)}) copy-start(f32[20,2]{0,1:T(2,128)} %param.15) | copy-start | bytes 484
  7.2 25.0 %copy-start.4 = (s32[2,2]{1,0:T(2,128)S(1)}, s32[2,2]{1,0:T(2,128)}, u32[]{:S(2)}) copy-start(s32[2,2]{1,0:T(2,128)} %param.16) | copy-start | bytes 52
  7.2 25.2 %copy-start.2 = (f32[16,2,2,256]{3,2,1,0:T(2,128)S(1)}, f32[16,2,2,256]{3,2,1,0:T(2,128)}, u32[]{:S(2)}) copy-start(f32[16,2,2,256]{3,2,1,0:T(2,128)} %param.17) | copy-start | bytes 196612
  7.2 105.9 %all-gather.2.cloned.1.call-start = ((), (), s32[]{:S(2)}) async-start(), calls=%async_computation.3 | async-start | bytes 5570560 | tf_op jit(solution)/shard_map/all_gather | solution.py:114
  12.9 13.9 %all-to-all-start = ((bf16[16,1,16]{2,1,0:T(2,128)(2,1)}), bf16[16,1,16]{2,1,0:T(2,128)(2,1)S(1)}, u32[]{:S(2)}, u32[]{:S(2)}) async-start(bf16[16,1,16]{2,1,0:T(2,128)(2,1)} %convert_element_type.79), calls=%async_computation | async-start | bytes 16384 | tf_op jit(solution)/shard_map/all_to_all | solution.py:80
  26.8 73.6 %all-to-all-start.1 = ((bf16[16,16,5120]{2,1,0:T(8,128)(2,1)}), bf16[16,16,5120]{2,1,0:T(8,128)(2,1)S(1)}, u32[]{:S(2)}, u32[]{:S(2)}) async-start(bf16[16,16,5120]{2,1,0:T(8,128)(2,1)} %bitcast.47), calls=%async_computation.2 | async-start | bytes 5242880 | tf_op jit(solution)/shard_map/all_to_all | solution.py:79
  32.1 208.5 %all-reduce.2.cloned.1.call-start = ((), (), s32[]{:S(2)}) async-start(), calls=%async_computation.5 | async-start | bytes 2097152 | tf_op jit(solution)/shard_map/psum | solution.py:129
  113.1 244.0 %reduce-scatter.2.cloned.1.call-start = ((), (), s32[]{:S(2)}) async-start(), calls=%async_computation.4 | async-start | bytes 5406720 | tf_op jit(solution)/shard_map/reduce_scatter | solution.py:125
  124.1 153.5 %copy-start.1 = (bf16[256,512]{1,0:T(8,128)(2,1)S(1)}, bf16[256,512]{1,0:T(8,128)(2,1)}, u32[]{:S(2)}) copy-start(bf16[256,512]{1,0:T(8,128)(2,1)} %param.21) | copy-start | bytes 786436
  273.1 12.7 %copy-start.3 = (f32[2,2]{1,0:T(2,128)}, f32[2,2]{1,0:T(2,128)S(1)}, u32[]{:S(2)}) copy-start(f32[2,2]{1,0:T(2,128)S(1)} %pmax.7) | copy-start | bytes 52
Sparse Core Ops, SparseCore 0:
  11.0 100.6 all-gather.1
  115.0 125.5 all-reduce.1
  243.5 113.5 reduce-scatter.1
where the time goes:
time: 368 us; the launch traced here: 365 us
  waiting for transfers between devices  186 us (51%)
  blocking collectives  69.4 us (19%)
  local copies, waits for them, and re-layouts  43.9 us (12%)
  matrix products  31.7 us (9%)
  between operations  13.9 us (4%)
  starting transfers between devices  13.1 us (4%)
  other arithmetic  6.94 us (2%)
    psum x1, waiting for transfers between devices, per_device(): lax.psum(jnp.einsum('rjkb,rjc->bjkc', chosen, up_grad_blocks, preferred_e...  113 us
    reduce_scatter x1, waiting for transfers between devices, per_device(): lax.psum_scatter(base_input + delta_input, 'col', scatter_dimension=1, ti...  71.3 us
    all_gather x1, blocking collectives, per_device(): lax.all_gather(delta.astype(jnp.bfloat16), 'tok', axis=0, tiled=True)  38.5 us
    pmax x1, blocking collectives, per_device(): block_scale = lax.pmax(local_max, 'tok')  30.9 us
    dot_general x1, matrix products, per_device(): lax.dot_general(up_grad, weight, (((1,), (1,)), ((), ())), preferred_elem...  11 us
    unnamed x16, local copies, waits for them, and re-layouts  9.64 us
    dot_general x1, matrix products, per_device(): base_up = jnp.dot(learn_x, weight, preferred_element_type=jnp.float32)  8.19 us
    all_to_all x1, starting transfers between devices, per_device(): lax.all_to_all(weight_slots.astype(jnp.bfloat16), 'tok', split_axis=0, co...  7.58 us
  transfers between devices with their start and end apart: 5, of which 3 were waited for; matrix products, arithmetic and copies ran while one was open for 22% of the time, Pallas kernels for 0%

commit v1 on v0

v1 whole, which is shorter than its diff:
```python
import functools

import jax
import jax.numpy as jnp
from jax import lax
from jax.experimental import pallas as pl
from jax.experimental.pallas import tpu as pltpu
from jax.sharding import PartitionSpec as P

BLK = 256
RESP = 64
STEP = 1000
D = 5120
NT = 16
NZ = 16
CAP = 16
ROWS = 128
COLS = 512
KS = D // 4
CROWS = 320
DCH = KS // NZ
GB = 144

beta_first = 0.9
beta_second = 0.999
step_rate = 0.01
adam_eps = 1e-08
scale_eps = 1e-06

MESH = pl.DeviceIdType.MESH
F32 = jnp.float32
BF16 = jnp.bfloat16


def dot_nn(a, b):
    return lax.dot_general(a, b, (((1,), (0,)), ((), ())), preferred_element_type=F32)


def dot_nt(a, b):
    return lax.dot_general(a, b, (((1,), (1,)), ((), ())), preferred_element_type=F32)


def dot_tn(a, b):
    return lax.dot_general(a, b, (((0,), (0,)), ((), ())), preferred_element_type=F32)


def is_same(a, b):
    return (1 - jnp.minimum(jnp.abs(a - b), 1)).astype(F32)


class Links:
    def __init__(self, send, recv):
        self.send, self.recv = send, recv
        self.sent = []

    def copy(self, src, dst, number, tok, col):
        return pltpu.make_async_remote_copy(
            src_ref=src,
            dst_ref=dst,
            send_sem=self.send.at[number],
            recv_sem=self.recv.at[number],
            device_id={"tok": tok, "col": col},
            device_id_type=MESH,
        )

    def start(self, src, dst, number, tok, col):
        made = self.copy(src, dst, number, tok, col)
        made.start()
        self.sent.append(made)

    def wait(self, dst, number):
        pltpu.make_async_copy(dst, dst, self.recv.at[number]).wait()

    def drain(self):
        for made in self.sent:
            made.wait_send()


class RingGather:
    def __init__(self, links, me, device, block, half):
        self.links, self.block, self.half, self.device = links, block, half, device
        self.me = me
        self.right, self.left, self.far = (me + 1) % 4, (me + 3) % 4, (me + 2) % 4

    def put(self, src, index, part, number, to):
        self.links.start(self.half(src, part), self.half(self.block(index), part), number, *self.device(to))

    def got(self, index, part, number):
        self.links.wait(self.half(self.block(index), part), number)

    def begin(self, src):
        self.put(src, self.me, 0, 0, self.right)
        self.put(src, self.me, 1, 1, self.left)
        self.put(src, self.me, 1, 2, self.right)
        self.put(src, self.me, 0, 3, self.left)

    def forward(self):
        self.got(self.left, 0, 0)
        self.put(self.block(self.left), self.left, 0, 4, self.right)
        self.got(self.right, 1, 1)
        self.put(self.block(self.right), self.right, 1, 5, self.left)

    def finish(self):
        self.got(self.left, 1, 2)
        self.got(self.right, 0, 3)
        self.got(self.far, 0, 4)
        self.got(self.far, 1, 5)


class RingReduce:
    def __init__(self, links, me, device, part, half, first, stage, second):
        self.links, self.part, self.half, self.device = links, part, half, device
        self.first, self.stage, self.second = first, stage, second
        self.me = me
        self.right, self.left, self.far = (me + 1) % 4, (me + 3) % 4, (me + 2) % 4

    def put(self, src, dst, number, to):
        self.links.start(src, dst, number, *self.device(to))

    def begin(self):
        self.put(self.half(self.part(self.far), 0), self.first.at[0], 0, self.right)
        self.put(self.half(self.part(self.far), 1), self.first.at[1], 1, self.left)
        self.put(self.half(self.part(self.right), 1), self.half(self.second.at[0], 1), 2, self.right)
        self.put(self.half(self.part(self.left), 0), self.half(self.second.at[1], 0), 3, self.left)

    def forward(self):
        self.links.wait(self.first.at[0], 0)
        self.stage[0] = (
            self.half(self.part(self.right), 0)[...].astype(F32) + self.first[0].astype(F32)
        ).astype(BF16)
        self.put(self.stage.at[0], self.half(self.second.at[0], 0), 4, self.right)
        self.links.wait(self.first.at[1], 1)
        self.stage[1] = (
            self.half(self.part(self.left), 1)[...].astype(F32) + self.first[1].astype(F32)
        ).astype(BF16)
        self.put(self.stage.at[1], self.half(self.second.at[1], 1), 5, self.left)

    def finish(self):
        self.links.wait(self.half(self.second.at[0], 1), 2)
        self.links.wait(self.half(self.second.at[1], 0), 3)
        self.links.wait(self.half(self.second.at[0], 0), 4)
        self.links.wait(self.half(self.second.at[1], 1), 5)

    def total(self, own):
        return own + (self.second[0].astype(F32) + self.second[1].astype(F32))


def rows_half(size):
    def half(ref, part):
        return ref.at[pl.ds(part * size, size), :]

    return half


def lanes_half(size):
    def half(ref, part):
        return ref.at[:, pl.ds(part * size, size)]

    return half


def g_half(ref, part):
    return ref.at[pl.ds(0, 64), :] if part == 0 else ref.at[pl.ds(64, GB - 64), :]


def kernel(
    lengths, scales, brows, rollout, route, codes, delta, adam_m, adam_v, gate_pre, hidden_grad,
    ig_out, gg_out, nd_out, nm_out, nv_out, ds_out, dc_out,
    u_send, u_buf, slope, w_buf, w_eff, x_buf, d_buf, g_buf, g_all,
    h_part, h_first, h_stage, h_second, hs_send, hs_buf,
    q_part, q_first, q_stage, q_second, r_part, r_first, r_stage, r_second,
    m_send, m_buf, z_own, z_give, z_take, z_send, z_recv, f_send, f_buf, chosen_rows,
    c_ss, c_rs, dy_ss, dy_rs, dx_ss, dx_rs, g_ss, g_rs, x_ss, x_rs, h_ss, h_rs,
    q_ss, q_rs, r_ss, r_rs, s_ss, s_rs, z_ss, z_rs, a_ss, a_rs,
):
    t = lax.axis_index("tok")
    c = lax.axis_index("col")
    y, x = t // 4, t % 4
    z, h = c // 2, c % 2

    def at_x(other):
        return y * 4 + other, c

    def at_y(other):
        return other * 4 + x, c

    codes_ring = RingGather(
        Links(c_ss, c_rs), x, at_x, lambda i: w_buf.at[pl.ds(i * CROWS, CROWS), :], rows_half(CROWS // 2)
    )
    codes_ring.begin(codes)
    w_buf[pl.ds(x * CROWS, CROWS), :] = codes[...]

    x_links = Links(x_ss, x_rs)
    for step in (1, 3, 2):
        to = (y + step) % 4
        x_links.start(
            rollout.at[pl.ds(64 * h, 64), pl.ds(pl.multiple_of(to * KS, KS), KS)],
            x_buf.at[pl.ds(y * ROWS + 64 * h, 64), :],
            step - 1,
            *at_y(to),
        )

    dy_ring = RingGather(
        Links(dy_ss, dy_rs), y, at_y, lambda i: d_buf.at[pl.ds(x * 64 + i * 16, 16), :], lanes_half(512)
    )
    own_delta = dy_ring.block(y)
    for j in range(2):
        for k in range(2):
            own_delta[:, (2 * j + k) * BLK : (2 * j + k + 1) * BLK] = delta[:, j, k, :].astype(BF16)
    dy_ring.begin(own_delta)

    def gate_rows(other):
        at = pl.ds(pl.multiple_of(other * CAP, CAP), CAP)
        v = gate_pre[at, :].astype(F32)
        hg = hidden_grad[at, :].astype(F32)
        s = 1.0 / (1.0 + jnp.exp(-v))
        slope[at, :] = hg * (s * (1.0 + v * (1.0 - s)))
        u_send[at, :] = (hg * (v * s)).astype(BF16)

    def a2a_copy(src, dst, number, other):
        return pltpu.make_async_remote_copy(
            src_ref=src.at[pl.ds(pl.multiple_of(other * CAP, CAP), CAP), :],
            dst_ref=dst.at[pl.ds(pl.multiple_of(t * CAP, CAP), CAP), :],
            send_sem=a_ss.at[number],
            recv_sem=a_rs.at[number],
            device_id={"tok": other, "col": c},
            device_id_type=MESH,
        )

    def gate_step(i, carry):
        other = (t + i) % NT
        gate_rows(other)
        a2a_copy(u_send, u_buf, 0, other).start()
        return carry

    lax.fori_loop(1, NT, gate_step, 0)
    gate_rows(t)
    own_cap = pl.ds(pl.multiple_of(t * CAP, CAP), CAP)
    u_buf[own_cap, :] = u_send[own_cap, :]

    lane = lax.broadcasted_iota(jnp.int32, (ROWS, ROWS), 1)
    row = lax.broadcasted_iota(jnp.int32, (ROWS, ROWS), 0)
    goes = route[...]
    onehot = jnp.where(goes == lane, 1.0, 0.0)
    lower = jnp.where(lane < row, 1.0, 0.0)
    earlier = dot_nn(lower.astype(BF16), onehot.astype(BF16))
    slot = jnp.sum(earlier * onehot, axis=1, keepdims=True)
    target = goes.astype(F32) * CAP + slot
    eye = jnp.where(lane == row, 1.0, 0.0).astype(BF16)
    target_row = dot_tn(jnp.broadcast_to(target, (ROWS, ROWS)).astype(BF16), eye)
    wide = lax.broadcasted_iota(jnp.int32, (ROWS, NT * CAP), 1).astype(F32)
    pick = jnp.where(wide == target, 1.0, 0.0).astype(BF16)
    row_id = lax.broadcasted_iota(jnp.int32, (ROWS, 1), 0)
    live = jnp.where(row_id < RESP, lengths[0], lengths[1])
    row_weight = jnp.where(row_id % RESP < live, RESP / live.astype(F32), 0.0)

    dy_ring.forward()
    codes_ring.forward()
    dy_ring.finish()
    dx_ring = RingGather(
        Links(dx_ss, dx_rs), x, at_x, lambda i: d_buf.at[pl.ds(i * 64, 64), :], rows_half(32)
    )
    dx_ring.begin(dx_ring.block(x))

    pltpu.make_async_copy(
        u_buf.at[pl.ds(0, 15 * CAP), :], u_buf.at[pl.ds(0, 15 * CAP), :], a_rs.at[0]
    ).wait()
    up_grad = (row_weight * dot_nn(pick, u_buf[...])).astype(BF16)
    g_ring = RingGather(Links(g_ss, g_rs), y, at_y, lambda i: g_buf.at[i], g_half)
    own_g = g_buf.at[y]
    own_g[0:ROWS, :] = up_grad
    own_g[ROWS:GB, :] = jnp.concatenate([target_row[0 : GB - ROWS, :]] * 4, axis=1).astype(BF16)
    g_ring.begin(own_g)

    def choose_rows(i, carry):
        at = pl.ds(pl.multiple_of(i * 32, 32), 32)
        picked = [jnp.zeros((32, BLK), BF16)] * 4
        for block in range(D // BLK):
            held = rollout[at, block * BLK : (block + 1) * BLK]
            for q in range(4):
                on = jnp.full((32, BLK), is_same(brows[q // 2, q % 2], block), F32).astype(BF16)
                picked[q] = picked[q] + on * held
        for q in range(4):
            chosen_rows[q, at, :] = picked[q]
        return carry

    lax.fori_loop(0, 4, choose_rows, 0)
    for j in range(2):
        for k in range(2):
            chosen = chosen_rows[2 * j + k]
            grad = dot_tn(chosen, up_grad[:, j * BLK : (j + 1) * BLK]).astype(BF16)
            for yy in range(4):
                for xx in range(4):
                    q_part[
                        64 * xx + 16 * yy : 64 * xx + 16 * yy + 16,
                        (2 * j + k) * BLK : (2 * j + k + 1) * BLK,
                    ] = grad[64 * yy + 16 * xx : 64 * yy + 16 * xx + 16, :]
    q_ring = RingReduce(
        Links(q_ss, q_rs), x, at_x, lambda i: q_part.at[pl.ds(i * 64, 64), :], rows_half(32),
        q_first, q_stage, q_second,
    )
    q_ring.begin()

    for step in (1, 3, 2):
        source = (y + 4 - step) % 4
        mine = x_buf.at[pl.ds(source * ROWS + 64 * h, 64), :]
        x_links.wait(mine, step - 1)
        x_links.start(mine, mine, 3 + step - 1, t, 2 * z + 1 - h)
    x_buf[pl.ds(y * ROWS, ROWS), :] = rollout[:, pl.ds(pl.multiple_of(y * KS, KS), KS)]

    dx_ring.forward()
    g_ring.forward()
    codes_ring.finish()
    dx_ring.finish()

    def weight_rows(index, carry):
        block = y * 5 + index // 4
        part = index % 4
        for j in range(2):
            scale = scales[block, j]
            on = [is_same(brows[j, k], block) for k in range(2)]
            for xx in range(4):
                at = pl.ds(pl.multiple_of(index * 64 + xx * 16, 16), 16)
                held = pl.ds(pl.multiple_of(64 * xx + 16 * part, 16), 16)
                value = w_buf[at, j * BLK : (j + 1) * BLK].astype(F32) * scale
                for k in range(2):
                    q = 2 * j + k
                    value = value + on[k] * d_buf[held, q * BLK : (q + 1) * BLK].astype(F32)
                w_eff[at, j * BLK : (j + 1) * BLK] = value.astype(BF16)
        return carry

    lax.fori_loop(0, 20, weight_rows, 0)

    g_ring.finish()
    for yy in range(4):
        g_all[ROWS * yy : ROWS * (yy + 1), :] = g_buf[yy, 0:ROWS, :]

    s_links = Links(s_ss, s_rs)
    give_rows = pl.ds(pl.multiple_of(256 * (1 - h), 256), 256)
    keep_rows = pl.ds(pl.multiple_of(256 * h, 256), 256)
    for part in range(4):
        at = pl.ds(part * 320, 320)
        z_give[at, :] = dot_nt(w_eff[at, :], g_all[give_rows, :]).astype(BF16)
        s_links.start(z_give.at[at, :], z_take.at[at, :], part, t, 2 * z + 1 - h)

    def keep_part(part, carry):
        at = pl.ds(pl.multiple_of(part * 320, 320), 320)
        z_own[at, :] = dot_nt(w_eff[at, :], g_all[keep_rows, :])
        return carry

    lax.fori_loop(0, 4, keep_part, 0)

    for step in (1, 3, 2):
        source = (y + 4 - step) % 4
        x_links.wait(x_buf.at[pl.ds(source * ROWS + 64 * (1 - h), 64), :], 3 + step - 1)

    def up_rows(i, carry):
        at = pl.ds(pl.multiple_of(i * ROWS, ROWS), ROWS)
        h_part[at, :] = dot_nn(x_buf[at, :], w_eff[...]).astype(BF16)
        return carry

    lax.fori_loop(0, 4, up_rows, 0)
    h_ring = RingReduce(
        Links(h_ss, h_rs), y, at_y, lambda i: h_part.at[pl.ds(i * ROWS, ROWS), :], rows_half(64),
        h_first, h_stage, h_second,
    )
    h_ring.begin()

    for part in range(4):
        s_links.wait(z_take.at[pl.ds(part * 320, 320), :], part)
    up_z, down_z = (z + 1) % NZ, (z + NZ - 1) % NZ

    def own_chunk(d, half):
        at = pl.ds(pl.multiple_of(d * DCH, DCH), DCH)
        lanes = slice(half * 128, half * 128 + 128)
        return z_own[at, lanes] + z_take[at, lanes].astype(F32)

    def ring_copy(way, half, step):
        return pltpu.make_async_remote_copy(
            src_ref=z_send.at[way, half, step],
            dst_ref=z_recv.at[way, half, step],
            send_sem=z_ss.at[(way * 2 + half) * 8 + step],
            recv_sem=z_rs.at[(way * 2 + half) * 8 + step],
            device_id={"tok": t, "col": 2 * (up_z if way == 0 else down_z) + h},
            device_id_type=MESH,
        )

    steps_of = (8, 7)

    def ring_step(step):
        for half in range(2):
            for way in range(2):
                if step >= steps_of[way]:
                    continue
                d = (z + 8 - step) % NZ if way == 0 else (z + NZ - 7 + step) % NZ
                value = own_chunk(d, half)
                if step > 0:
                    ring_copy(way, half, step - 1).wait_recv()
                    value = value + z_recv[way, half, step - 1].astype(F32)
                z_send[way, half, step] = value.astype(BF16)
                ring_copy(way, half, step).start()

    ring_step(0)
    q_ring.forward()
    ring_step(1)
    h_ring.forward()
    ring_step(2)
    q_ring.finish()
    r_part[...] = q_ring.total(q_part[pl.ds(x * 64, 64), :].astype(F32)).astype(BF16)
    r_ring = RingReduce(
        Links(r_ss, r_rs), y, at_y, lambda i: r_part.at[pl.ds(i * 16, 16), :], lanes_half(512),
        r_first, r_stage, r_second,
    )
    r_ring.begin()
    ring_step(3)
    h_ring.finish()
    up_value = h_ring.total(h_part[pl.ds(y * ROWS, ROWS), :].astype(F32)) * row_weight
    slot_row = lax.broadcasted_iota(jnp.int32, (NT * CAP, ROWS), 0).astype(F32)
    put_slots = jnp.where(slot_row == target_row[0:1, :], 1.0, 0.0).astype(BF16)
    hs_send[...] = dot_nn(put_slots, up_value.astype(BF16)).astype(BF16)

    def h_step(i, carry):
        a2a_copy(hs_send, hs_buf, 1, (t + i) % NT).start()
        return carry

    lax.fori_loop(1, NT, h_step, 0)
    hs_buf[own_cap, :] = hs_send[own_cap, :]
    ring_step(4)
    r_ring.forward()
    ring_step(5)
    r_ring.finish()
    gradient = r_ring.total(r_part[pl.ds(pl.multiple_of(y * 16, 16), 16), :].astype(F32))

    tops = []
    for j in range(2):
        for k in range(2):
            q = 2 * j + k
            g = gradient[:, q * BLK : (q + 1) * BLK]
            new_m = beta_first * adam_m[:, j, k, :] + (1.0 - beta_first) * g
            new_v = beta_second * adam_v[:, j, k, :] + (1.0 - beta_second) * g * g
            corrected_m = new_m / (1.0 - beta_first**STEP)
            corrected_v = new_v / (1.0 - beta_second**STEP)
            new_delta = delta[:, j, k, :] - step_rate * corrected_m / (
                jnp.sqrt(corrected_v) + adam_eps
            )
            nm_out[:, j, k, :] = new_m
            nv_out[:, j, k, :] = new_v
            nd_out[:, j, k, :] = new_delta
            tops.append(jnp.max(jnp.abs(new_delta)))
    tile_row = lax.broadcasted_iota(jnp.int32, (8, 128), 0)
    tile = jnp.zeros((8, 128), F32)
    for q in range(4):
        tile = jnp.where(tile_row == q, tops[q], tile)
    m_send[...] = tile
    m_buf[t] = tile

    def m_copy(other):
        return pltpu.make_async_remote_copy(
            src_ref=m_send,
            dst_ref=m_buf.at[t],
            send_sem=a_ss.at[2],
            recv_sem=a_rs.at[2],
            device_id={"tok": other, "col": c},
            device_id_type=MESH,
        )

    def m_step(i, carry):
        m_copy((t + i) % NT).start()
        return carry

    lax.fori_loop(1, NT, m_step, 0)
    ring_step(6)

    pltpu.make_async_copy(
        hs_buf.at[pl.ds(0, 15 * CAP), :], hs_buf.at[pl.ds(0, 15 * CAP), :], a_rs.at[1]
    ).wait()
    gg_out[...] = (slope[...] * hs_buf[...].astype(F32)).astype(BF16)
    ring_step(7)

    pltpu.make_async_copy(m_buf.at[pl.ds(0, 15)], m_buf.at[pl.ds(0, 15)], a_rs.at[2]).wait()
    top = jnp.max(m_buf[...], axis=0)
    for j in range(2):
        for k in range(2):
            q = 2 * j + k
            scale = jnp.max(top[q : q + 1, :])
            ds_out[j, k] = scale
            dc_out[:, j, k, :] = (nd_out[:, j, k, :] / (scale + scale_eps)).astype(BF16)

    g_rows = []
    halves = []
    for half in range(2):
        ring_copy(0, half, 7).wait_recv()
        ring_copy(1, half, 6).wait_recv()
        total = own_chunk(z, half) + (
            z_recv[0, half, 7].astype(F32) + z_recv[1, half, 6].astype(F32)
        )
        halves.append(total.astype(BF16))
        g_rows.append(g_buf[2 * h + half, ROWS : ROWS + 16, 0:128].astype(F32)[0:1, :])
    chunk = jnp.concatenate(halves, axis=1)
    chunk = jnp.concatenate([chunk, jnp.zeros((128 - DCH, 256), BF16)], axis=0)
    wanted = jnp.concatenate(g_rows, axis=1)
    spot = lax.broadcasted_iota(jnp.int32, (2 * NT * CAP, 256), 0)
    side = lax.broadcasted_iota(jnp.int32, (2 * NT * CAP, 256), 1) // 128
    slot_of = ((spot // 32) * 16 + spot % 16).astype(F32)
    put_both = jnp.where((slot_of == wanted) & (side == (spot // 16) % 2), 1.0, 0.0).astype(BF16)
    f_send[...] = dot_nt(put_both, chunk).astype(BF16)
    to_col = 8 * y + z // 2

    def f_copy(other):
        return pltpu.make_async_remote_copy(
            src_ref=f_send.at[pl.ds(pl.multiple_of(other * 32, 32), 32), :],
            dst_ref=f_buf.at[z % 2, x * 2 + h],
            send_sem=a_ss.at[3],
            recv_sem=a_rs.at[3],
            device_id={"tok": other, "col": to_col},
            device_id_type=MESH,
        )

    stays = to_col == c

    @pl.when(stays)
    def _():
        f_buf[z % 2, x * 2 + h] = f_send[pl.ds(pl.multiple_of(t * 32, 32), 32), :]

    @pl.when(jnp.logical_not(stays))
    def _():
        f_copy(t).start()

    def f_step(i, carry):
        f_copy((t + i) % NT).start()
        return carry

    lax.fori_loop(1, NT, f_step, 0)

    from_row = c // 8
    mine_too = (from_row == y) & ((c % 8) == z // 2)

    @pl.when(mine_too)
    def _():
        pltpu.make_async_copy(
            f_send.at[pl.ds(0, 480), :], f_send.at[pl.ds(0, 480), :], a_rs.at[3]
        ).wait()

    @pl.when(jnp.logical_not(mine_too))
    def _():
        pltpu.make_async_copy(f_send, f_send, a_rs.at[3]).wait()

    lane_in = lax.broadcasted_iota(jnp.int32, (128, 256), 0)
    lane_out = lax.broadcasted_iota(jnp.int32, (128, 256), 1)
    place = [
        jnp.where((lane_in < DCH) & (lane_out == lane_in + DCH * side_of), 1.0, 0.0).astype(BF16)
        for side_of in range(2)
    ]
    for xx in range(4):
        for hh in range(2):
            got = dot_nn(f_buf[0, xx * 2 + hh], place[0]) + dot_nn(f_buf[1, xx * 2 + hh], place[1])
            got = got[:, 0:160].astype(BF16)
            for part in range(2):
                sender = 4 * (2 * hh + part) + xx
                ig_out[16 * sender : 16 * sender + 16, :] = got[16 * part : 16 * part + 16, :]

    for links in (
        codes_ring.links, x_links, dy_ring.links, dx_ring.links, g_ring.links,
        q_ring.links, r_ring.links, h_ring.links, s_links,
    ):
        links.drain()
    for way in range(2):
        for half in range(2):
            for step in range(steps_of[way]):
                ring_copy(way, half, step).wait_send()
    for number in range(2):
        pltpu.make_async_copy(
            u_buf.at[pl.ds(0, 15 * CAP), :], u_buf.at[pl.ds(0, 15 * CAP), :], a_ss.at[number]
        ).wait()
    pltpu.make_async_copy(m_buf.at[pl.ds(0, 15)], m_buf.at[pl.ds(0, 15)], a_ss.at[2]).wait()

    @pl.when(stays)
    def _():
        pltpu.make_async_copy(
            f_send.at[pl.ds(0, 480), :], f_send.at[pl.ds(0, 480), :], a_ss.at[3]
        ).wait()

    @pl.when(jnp.logical_not(stays))
    def _():
        pltpu.make_async_copy(f_send, f_send, a_ss.at[3]).wait()


def per_device(
    rollout, lengths, route, up_codes, up_scales, block_rows, delta, adam_m, adam_v, gate_pre, hidden_grad
):
    vmem = pl.BlockSpec(memory_space=pltpu.VMEM)
    smem = pl.BlockSpec(memory_space=pltpu.SMEM)
    dma = pltpu.SemaphoreType.DMA

    def bf(*shape):
        return pltpu.VMEM(shape, BF16)

    def fl(*shape):
        return pltpu.VMEM(shape, F32)

    scratch = [
        bf(256, COLS), bf(256, COLS), fl(256, COLS), bf(KS, COLS), bf(KS, COLS), bf(4 * ROWS, KS),
        bf(256, 1024), bf(4, GB, COLS), bf(4 * ROWS, COLS),
        bf(4 * ROWS, COLS), bf(2, 64, COLS), bf(2, 64, COLS), bf(2, ROWS, COLS),
        bf(256, COLS), bf(256, COLS),
        bf(256, 1024), bf(2, 32, 1024), bf(2, 32, 1024), bf(2, 64, 1024),
        bf(64, 1024), bf(2, 16, 512), bf(2, 16, 512), bf(2, 16, 1024),
        fl(8, 128), fl(NT, 8, 128), fl(KS, 256), bf(KS, 256), bf(KS, 256),
        bf(2, 2, 8, DCH, 128), bf(2, 2, 8, DCH, 128), bf(512, 128), bf(2, 8, 32, 128), bf(4, ROWS, BLK),
        dma((6,)), dma((6,)), dma((6,)), dma((6,)), dma((6,)), dma((6,)), dma((6,)), dma((6,)),
        dma((6,)), dma((6,)), dma((6,)), dma((6,)), dma((6,)), dma((6,)), dma((6,)), dma((6,)),
        dma((4,)), dma((4,)), dma((32,)), dma((32,)), dma((4,)), dma((4,)),
    ]
    block = jax.ShapeDtypeStruct(delta.shape, F32)
    return pl.pallas_call(
        kernel,
        out_shape=(
            jax.ShapeDtypeStruct((256, 160), BF16),
            jax.ShapeDtypeStruct((256, COLS), BF16),
            block,
            block,
            block,
            jax.ShapeDtypeStruct((2, 2), F32),
            jax.ShapeDtypeStruct(delta.shape, BF16),
        ),
        in_specs=[smem] * 3 + [vmem] * 8,
        out_specs=(vmem, vmem, vmem, vmem, vmem, smem, vmem),
        scratch_shapes=scratch,
        compiler_params=pltpu.CompilerParams(has_side_effects=True, vmem_limit_bytes=48 * 1024 * 1024),
        cost_estimate=pl.CostEstimate(flops=3 * 10**9, bytes_accessed=4 * 10**6, transcendentals=0),
    )(
        lengths, up_scales, block_rows, rollout, route, up_codes, delta, adam_m, adam_v, gate_pre, hidden_grad
    )


def solution(mesh):
    placed = (
        P("tok", None),
        P("tok"),
        P("tok", None),
        P("tok", "col"),
        P(None, "col"),
        P("col", None),
        P("tok", "col", None, None),
        P("tok", "col", None, None),
        P("tok", "col", None, None),
        P("tok", "col"),
        P("tok", "col"),
    )
    return jax.shard_map(
        per_device,
        mesh=mesh,
        in_specs=placed,
        out_specs=(
            P("tok", "col"),
            P("tok", "col"),
            P("tok", "col", None, None),
            P("tok", "col", None, None),
            P("tok", "col", None, None),
            P("col", None),
            P("tok", "col", None, None),
        ),
        check_vma=False,
    )
```

time: 368 us -> 121 us (0.33)
  waiting for transfers between devices: 186 us -> 0 us
  Pallas kernels: 0 us -> 106 us
  blocking collectives: 69.4 us -> 0 us
  matrix products: 31.7 us -> 0 us
  local copies, waits for them, and re-layouts: 43.9 us -> 14.1 us
  between operations: 13.9 us -> 0.66 us
  starting transfers between devices: 13.1 us -> 0 us
  other arithmetic: 6.94 us -> 0 us
    psum x1 -> x0, waiting for transfers between devices: 113 us -> none  [per_device(): lax.psum(jnp.einsum('rjkb,rjc->bjkc', chosen, up_grad_blocks, preferred_e...]
    pallas_call x0 -> x1, Pallas kernels: none -> 106 us  [per_device(): pl.pallas_call(kernel, out_shape=(jax.ShapeDtypeStruct((256, 160), BF16),...]
    reduce_scatter x1 -> x0, waiting for transfers between devices: 71.3 us -> none  [per_device(): lax.psum_scatter(base_input + delta_input, 'col', scatter_dimension=1, ti...]
    all_gather x1 -> x0, blocking collectives: 38.5 us -> none  [per_device(): lax.all_gather(delta.astype(jnp.bfloat16), 'tok', axis=0, tiled=True)]
    dot_general x7 -> x0, matrix products: 31.7 us -> none  [the longest x1 11 us: per_device(): lax.dot_general(up_grad, weight, (((1,), (1,)), ((), ())), preferred_elem...]
    pmax x1 -> x0, blocking collectives: 30.9 us -> none  [per_device(): block_scale = lax.pmax(local_max, 'tok')]
    all_to_all x2 -> x0, starting transfers between devices: 12.9 us -> none  [the longest x1 7.58 us: per_device(): lax.all_to_all(weight_slots.astype(jnp.bfloat16), 'tok', split_axis=0, co...]
    another operation x2 -> x0, local copies, waits for them, and re-layouts: 7.06 us -> none  [per_device(): learn_x.reshape(rows_learn, block_total, BLK)]
  transfers between devices with their start and end apart: 5 -> 0, of which waited for: 3 -> 0; matrix products, arithmetic and copies ran while one was open for 22% -> 0% of each run, Pallas kernels for 0% -> 0%
where the time goes in v1:
time: 121 us; the launch traced here: 120 us
  Pallas kernels  106 us (88%)
  local copies, waits for them, and re-layouts  14.1 us (12%)
    pallas_call x1, Pallas kernels, per_device(): pl.pallas_call(kernel, out_shape=(jax.ShapeDtypeStruct((256, 160), BF16),...  106 us
    unnamed x26, local copies, waits for them, and re-layouts  13.3 us

profile of v1, /device:TPU:1, one launch (start us, length us, event | category | flops | bytes accessed | tf_op | source)
XLA Modules:
  0.0 120.2 jit_solution(13506167176979891406)
XLA Ops:
  0.6 0.8 copy.18.scales
  1.4 0.8 copy.19.route
  2.2 0.0 copy-start
  2.2 1.3 %copy-done = bf16[128,5120]{1,0:T(8,128)(2,1)S(1)} copy-done((bf16[128,5120]{1,0:T(8,128)(2,1)S(1)}, bf16[128,5120]{1,0:T(8,128)(2,1)}, u32[]{:S(2)}) %copy-start) | copy-done | bytes 1310744
  3.5 0.0 copy-start.1
  3.5 1.0 copy-done.1
  4.5 0.0 copy-start.2
  4.5 0.9 copy-done.2
  5.4 0.0 copy-start.3
  5.4 0.9 copy-done.3
  6.4 0.0 copy-start.4
  6.4 0.8 copy-done.4
  7.2 0.0 copy-start.5
  7.2 0.8 copy-done.5
  8.0 0.0 copy-start.6
  8.0 0.8 copy-done.6
  8.9 0.0 copy-start.7
  8.9 0.7 copy-done.7
  9.6 0.0 copy-start.8
  9.6 0.7 copy-done.8
  10.2 105.5 %shard_map.162 = (bf16[256,160]{1,0:T(8,128)(2,1)S(1)}, bf16[256,512]{1,0:T(8,128)(2,1)S(1)}, f32[16,2,2,256]{3,2,1,0:T(2,128)S(1)}, f32[16,2,2,256]{3,2,1,0:T(2...) custom-call(s32[2]{0:T(128)S(1)} %copy-done.8, ...), custom_call_target="tpu_custom_call" | custom-call | flops 3000000000 | bytes 4000000 | tf_op jit(solution)/shard_map/pallas_call | solution.py:615
  115.7 0.7 copy.20
  116.5 0.7 copy.27
  117.2 0.6 copy.28
  117.8 0.6 copy.29
  118.4 0.6 copy.30
  119.1 0.6 copy.31
  119.6 0.6 copy.32
Async XLA Ops:
  2.2 1.3 %copy-start = (bf16[128,5120]{1,0:T(8,128)(2,1)S(1)}, bf16[128,5120]{1,0:T(8,128)(2,1)}, u32[]{:S(2)}) copy-start(bf16[128,5120]{1,0:T(8,128)(2,1)} %rollout.1) | copy-start | bytes 3932164
  3.5 1.0 copy-start.1
  4.5 0.9 copy-start.2
  5.4 0.9 copy-start.3
  6.4 0.8 copy-start.4
  7.2 0.8 copy-start.5
  8.0 0.8 copy-start.6
  8.9 0.7 copy-start.7
  9.6 0.7 copy-start.8

commit v2 on v1

v2 whole, which is shorter than its diff:
```python
import functools

import jax
import jax.numpy as jnp
from jax import lax
from jax.experimental import pallas as pl
from jax.experimental.pallas import tpu as pltpu
from jax.sharding import PartitionSpec as P

BLK = 256
VLIM = 62
RESP = 64
STEP = 1000
D = 5120
NT = 16
NZ = 16
CAP = 16
ROWS = 128
COLS = 512
KS = D // 4
CROWS = 320
DCH = KS // NZ
GB = 144

beta_first = 0.9
beta_second = 0.999
step_rate = 0.01
adam_eps = 1e-08
scale_eps = 1e-06

MESH = pl.DeviceIdType.MESH
F32 = jnp.float32
BF16 = jnp.bfloat16


def dot_nn(a, b):
    return lax.dot_general(a, b, (((1,), (0,)), ((), ())), preferred_element_type=F32)


def dot_nt(a, b):
    return lax.dot_general(a, b, (((1,), (1,)), ((), ())), preferred_element_type=F32)


def dot_tn(a, b):
    return lax.dot_general(a, b, (((0,), (0,)), ((), ())), preferred_element_type=F32)


def is_same(a, b):
    return (1 - jnp.minimum(jnp.abs(a - b), 1)).astype(F32)


class Links:
    def __init__(self, send, recv):
        self.send, self.recv = send, recv
        self.sent = []

    def copy(self, src, dst, number, tok, col):
        return pltpu.make_async_remote_copy(
            src_ref=src,
            dst_ref=dst,
            send_sem=self.send.at[number],
            recv_sem=self.recv.at[number],
            device_id={"tok": tok, "col": col},
            device_id_type=MESH,
        )

    def start(self, src, dst, number, tok, col):
        made = self.copy(src, dst, number, tok, col)
        made.start()
        self.sent.append(made)

    def wait(self, dst, number):
        pltpu.make_async_copy(dst, dst, self.recv.at[number]).wait()

    def drain(self):
        for made in self.sent:
            made.wait_send()


class RingGather:
    def __init__(self, links, me, device, block, half):
        self.links, self.block, self.half, self.device = links, block, half, device
        self.me = me
        self.right, self.left, self.far = (me + 1) % 4, (me + 3) % 4, (me + 2) % 4

    def put(self, src, index, part, number, to):
        self.links.start(self.half(src, part), self.half(self.block(index), part), number, *self.device(to))

    def got(self, index, part, number):
        self.links.wait(self.half(self.block(index), part), number)

    def begin(self, src):
        self.put(src, self.me, 0, 0, self.right)
        self.put(src, self.me, 1, 1, self.left)
        self.put(src, self.me, 1, 2, self.right)
        self.put(src, self.me, 0, 3, self.left)

    def forward(self):
        self.got(self.left, 0, 0)
        self.put(self.block(self.left), self.left, 0, 4, self.right)
        self.got(self.right, 1, 1)
        self.put(self.block(self.right), self.right, 1, 5, self.left)

    def finish(self):
        self.got(self.left, 1, 2)
        self.got(self.right, 0, 3)
        self.got(self.far, 0, 4)
        self.got(self.far, 1, 5)


class RingReduce:
    def __init__(self, links, me, device, part, half, first, stage, second):
        self.links, self.part, self.half, self.device = links, part, half, device
        self.first, self.stage, self.second = first, stage, second
        self.me = me
        self.right, self.left, self.far = (me + 1) % 4, (me + 3) % 4, (me + 2) % 4

    def put(self, src, dst, number, to):
        self.links.start(src, dst, number, *self.device(to))

    def begin(self):
        self.put(self.half(self.part(self.far), 0), self.first.at[0], 0, self.right)
        self.put(self.half(self.part(self.far), 1), self.first.at[1], 1, self.left)
        self.put(self.half(self.part(self.right), 1), self.half(self.second.at[0], 1), 2, self.right)
        self.put(self.half(self.part(self.left), 0), self.half(self.second.at[1], 0), 3, self.left)

    def forward(self):
        self.links.wait(self.first.at[0], 0)
        self.stage[0] = (
            self.half(self.part(self.right), 0)[...].astype(F32) + self.first[0].astype(F32)
        ).astype(BF16)
        self.put(self.stage.at[0], self.half(self.second.at[0], 0), 4, self.right)
        self.links.wait(self.first.at[1], 1)
        self.stage[1] = (
            self.half(self.part(self.left), 1)[...].astype(F32) + self.first[1].astype(F32)
        ).astype(BF16)
        self.put(self.stage.at[1], self.half(self.second.at[1], 1), 5, self.left)

    def finish(self):
        self.links.wait(self.half(self.second.at[0], 1), 2)
        self.links.wait(self.half(self.second.at[1], 0), 3)
        self.links.wait(self.half(self.second.at[0], 0), 4)
        self.links.wait(self.half(self.second.at[1], 1), 5)

    def total(self, own):
        return own + (self.second[0].astype(F32) + self.second[1].astype(F32))


def rows_half(size):
    def half(ref, part):
        return ref.at[pl.ds(part * size, size), :]

    return half


def lanes_half(size):
    def half(ref, part):
        return ref.at[:, pl.ds(part * size, size)]

    return half


def g_half(ref, part):
    return ref.at[pl.ds(0, 64), :] if part == 0 else ref.at[pl.ds(64, GB - 64), :]


def kernel(
    lengths_h, scales_h, brows_h, rollout_h, route_h, codes_h, delta_h, m_h, v_h, gate_h, hidden_h,
    ig_out, gg_out, nd_out, nm_out, nv_out, ds_out, dc_out,
    lengths, scales, brows, rollout, route, delta, adam_m, adam_v, gate_pre, hidden_grad,
    u_send, u_buf, slope, w_buf, w_eff, x_buf, d_buf, g_buf, g_all,
    h_part, h_first, h_stage, h_second, hs_send, hs_buf,
    q_part, q_first, q_stage, q_second, r_part, r_first, r_stage, r_second,
    m_send, m_buf, z_own, z_give, z_take, z_send, z_recv, f_send, f_buf, e_send, e_buf, chosen_rows, put_both,
    in_s, c_ss, c_rs, dy_ss, dy_rs, dx_ss, dx_rs, g_ss, g_rs, x_ss, x_rs, h_ss, h_rs,
    q_ss, q_rs, r_ss, r_rs, s_ss, s_rs, z_ss, z_rs, a_ss, a_rs, e_ss, e_rs,
):
    t = lax.axis_index("tok")
    c = lax.axis_index("col")
    y, x = t // 4, t % 4
    z, h = c // 2, c % 2
    sibling = 2 * z + 1 - h

    def at_x(other):
        return y * 4 + other, c

    def at_y(other):
        return other * 4 + x, c

    own_codes = w_buf.at[pl.ds(x * CROWS, CROWS), :]
    pairs = (
        (hidden_h, hidden_grad), (gate_h, gate_pre), (delta_h, delta), (codes_h, own_codes),
        (route_h, route), (lengths_h, lengths), (rollout_h, rollout), (brows_h, brows),
        (scales_h, scales), (m_h, adam_m), (v_h, adam_v),
    )
    loads = [pltpu.make_async_copy(src, dst, in_s.at[i]) for i, (src, dst) in enumerate(pairs)]
    for load in loads:
        load.start()

    def chunk_of(chip, row):
        return (chip + 22 - 4 * row) % NZ

    def end_of(row):
        chunk = chunk_of(z, row)
        return 2 * (4 * row + chunk // 4) + (chunk // 2) % 2

    def start_of(number):
        row = z // 4
        chunk = 4 * (z % 4) + 2 * h + number // 2
        return 2 * ((chunk + 10 + 4 * row) % NZ) + number % 2

    barrier = pltpu.get_barrier_semaphore()

    def greet(tok, col):
        pl.semaphore_signal(barrier, inc=1, device_id={"tok": tok, "col": col}, device_id_type=MESH)

    def greet_plane(i, carry):
        greet((t + i) % NT, c)
        return carry

    lax.fori_loop(1, NT, greet_plane, 0)
    greet(t, sibling)
    for distance in (1, 2, NZ - 2, NZ - 1):
        greet(t, 2 * ((z + distance) % NZ) + h)
    for number in range(4):
        for other in (end_of(number), start_of(number)):

            @pl.when(other != c)
            def _():
                greet(t, other)

    stays = end_of(z // 4) == c

    loads[0].wait()
    loads[1].wait()

    def gate_rows(i, carry):
        at = pl.ds(pl.multiple_of(i * 32, 32), 32)
        v = gate_pre[at, :].astype(F32)
        hg = hidden_grad[at, :].astype(F32)
        s = 1.0 / (1.0 + jnp.exp(-v))
        slope[at, :] = hg * (s * (1.0 + v * (1.0 - s)))
        u_send[at, :] = (hg * (v * s)).astype(BF16)
        return carry

    lax.fori_loop(0, 8, gate_rows, 0)

    dy_ring = RingGather(
        Links(dy_ss, dy_rs), y, at_y, lambda i: d_buf.at[pl.ds(x * 64 + i * 16, 16), :], lanes_half(512)
    )
    own_delta = dy_ring.block(y)
    loads[2].wait()
    for j in range(2):
        for k in range(2):
            own_delta[:, (2 * j + k) * BLK : (2 * j + k + 1) * BLK] = delta[:, j, k, :].astype(BF16)
    loads[3].wait()

    pl.semaphore_wait(barrier, jnp.where(stays, 26, 28))

    def a2a_copy(src, dst, number, other):
        return pltpu.make_async_remote_copy(
            src_ref=src.at[pl.ds(pl.multiple_of(other * CAP, CAP), CAP), :],
            dst_ref=dst.at[pl.ds(pl.multiple_of(t * CAP, CAP), CAP), :],
            send_sem=a_ss.at[number],
            recv_sem=a_rs.at[number],
            device_id={"tok": other, "col": c},
            device_id_type=MESH,
        )

    def u_step(i, carry):
        a2a_copy(u_send, u_buf, 0, (t + i) % NT).start()
        return carry

    lax.fori_loop(1, NT, u_step, 0)
    own_cap = pl.ds(pl.multiple_of(t * CAP, CAP), CAP)
    u_buf[own_cap, :] = u_send[own_cap, :]
    dy_ring.begin(own_delta)

    codes_ring = RingGather(
        Links(c_ss, c_rs), x, at_x, lambda i: w_buf.at[pl.ds(i * CROWS, CROWS), :], rows_half(CROWS // 2)
    )
    codes_ring.begin(own_codes)

    for load in loads[4:]:
        load.wait()
    lane = lax.broadcasted_iota(jnp.int32, (ROWS, ROWS), 1)
    row = lax.broadcasted_iota(jnp.int32, (ROWS, ROWS), 0)
    eye = jnp.where(lane == row, 1.0, 0.0).astype(BF16)
    route_rows = jnp.broadcast_to(route[...].astype(F32), (ROWS, ROWS)).astype(BF16)
    goes = dot_nt(eye, route_rows)
    onehot = jnp.where(goes == lane.astype(F32), 1.0, 0.0)
    lower = jnp.where(lane < row, 1.0, 0.0)
    earlier = dot_nn(lower.astype(BF16), onehot.astype(BF16))
    slot = jnp.sum(earlier * onehot, axis=1, keepdims=True)
    target = goes * CAP + slot
    target_row = dot_tn(target.astype(BF16), eye)
    wide = lax.broadcasted_iota(jnp.int32, (ROWS, NT * CAP), 1).astype(F32)
    pick = jnp.where(wide == target[:, 0:1], 1.0, 0.0).astype(BF16)
    slot_row = lax.broadcasted_iota(jnp.int32, (NT * CAP, ROWS), 0).astype(F32)
    put_slots = jnp.where(slot_row == target_row[0:1, :], 1.0, 0.0).astype(BF16)
    row_id = lax.broadcasted_iota(jnp.int32, (ROWS, 1), 0)
    live = jnp.where(row_id < RESP, lengths[0], lengths[1])
    row_weight = jnp.where(row_id % RESP < live, RESP / live.astype(F32), 0.0)

    pltpu.make_async_copy(
        u_buf.at[pl.ds(0, 15 * CAP), :], u_buf.at[pl.ds(0, 15 * CAP), :], a_rs.at[0]
    ).wait()
    up_grad = (row_weight * dot_nn(pick, u_buf[...])).astype(BF16)
    g_ring = RingGather(Links(g_ss, g_rs), y, at_y, lambda i: g_buf.at[i], g_half)
    own_g = g_buf.at[y]
    own_g[0:ROWS, :] = up_grad
    own_g[ROWS:GB, :] = jnp.concatenate([target_row[0 : GB - ROWS, :]] * 4, axis=1).astype(BF16)
    g_ring.begin(own_g)

    dy_ring.forward()
    codes_ring.forward()
    dy_ring.finish()
    dx_ring = RingGather(
        Links(dx_ss, dx_rs), x, at_x, lambda i: d_buf.at[pl.ds(i * 64, 64), :], rows_half(32)
    )
    dx_ring.begin(dx_ring.block(x))
    g_ring.forward()

    x_links = Links(x_ss, x_rs)
    for step in (1, 3, 2):
        to = (y + step) % 4
        x_links.start(
            rollout.at[pl.ds(64 * h, 64), pl.ds(pl.multiple_of(to * KS, KS), KS)],
            x_buf.at[pl.ds(y * ROWS + 64 * h, 64), :],
            step - 1,
            *at_y(to),
        )

    def choose_rows(i, carry):
        at = pl.ds(pl.multiple_of(i * 32, 32), 32)
        picked = [jnp.zeros((32, BLK), BF16)] * 4
        for block in range(D // BLK):
            held = rollout[at, block * BLK : (block + 1) * BLK]
            for q in range(4):
                on = jnp.full((32, BLK), is_same(brows[q // 2, q % 2], block), F32).astype(BF16)
                picked[q] = picked[q] + on * held
        for q in range(4):
            chosen_rows[q, at, :] = picked[q]
        return carry

    lax.fori_loop(0, 4, choose_rows, 0)
    for j in range(2):
        for k in range(2):
            chosen = chosen_rows[2 * j + k]
            grad = dot_tn(chosen, up_grad[:, j * BLK : (j + 1) * BLK]).astype(BF16)
            for yy in range(4):
                for xx in range(4):
                    q_part[
                        64 * xx + 16 * yy : 64 * xx + 16 * yy + 16,
                        (2 * j + k) * BLK : (2 * j + k + 1) * BLK,
                    ] = grad[64 * yy + 16 * xx : 64 * yy + 16 * xx + 16, :]
    q_ring = RingReduce(
        Links(q_ss, q_rs), x, at_x, lambda i: q_part.at[pl.ds(i * 64, 64), :], rows_half(32),
        q_first, q_stage, q_second,
    )
    q_ring.begin()
    x_buf[pl.ds(y * ROWS, ROWS), :] = rollout[:, pl.ds(pl.multiple_of(y * KS, KS), KS)]

    dx_ring.forward()
    dx_ring.finish()
    g_ring.finish()
    for yy in range(4):
        g_all[ROWS * yy : ROWS * (yy + 1), :] = g_buf[yy, 0:ROWS, :]

    def weight_rows(index, carry):
        block = y * 5 + index // 4
        part = index % 4
        for j in range(2):
            scale = scales[j, block]
            on = [is_same(brows[j, k], block) for k in range(2)]
            for xx in range(4):
                at = pl.ds(pl.multiple_of(index * 64 + xx * 16, 16), 16)
                held = pl.ds(pl.multiple_of(64 * xx + 16 * part, 16), 16)
                value = w_buf[at, j * BLK : (j + 1) * BLK].astype(F32) * scale
                for k in range(2):
                    q = 2 * j + k
                    value = value + on[k] * d_buf[held, q * BLK : (q + 1) * BLK].astype(F32)
                w_eff[at, j * BLK : (j + 1) * BLK] = value.astype(BF16)
        return carry

    s_links = Links(s_ss, s_rs)
    give_rows = pl.ds(pl.multiple_of(256 * (1 - h), 256), 256)
    keep_rows = pl.ds(pl.multiple_of(256 * h, 256), 256)
    for order, part in enumerate((x, codes_ring.left, codes_ring.right, codes_ring.far)):
        if order == 1:
            codes_ring.got(part, 1, 2)
        if order == 2:
            codes_ring.got(part, 0, 3)
        if order == 3:
            codes_ring.got(part, 0, 4)
            codes_ring.got(part, 1, 5)
        lax.fori_loop(5 * part, 5 * part + 5, weight_rows, 0)
        at = pl.ds(pl.multiple_of(part * CROWS, CROWS), CROWS)
        z_give[at, :] = dot_nt(w_eff[at, :], g_all[give_rows, :]).astype(BF16)
        s_links.start(z_give.at[at, :], z_take.at[at, :], order, t, sibling)
        z_own[at, :] = dot_nt(w_eff[at, :], g_all[keep_rows, :])

    wanted = jnp.concatenate(
        [g_buf[2 * h + half, ROWS : ROWS + 16, 0:128].astype(F32)[0:1, :] for half in range(2)], axis=1
    )
    spot = lax.broadcasted_iota(jnp.int32, (2 * NT * CAP, 256), 0)
    side = lax.broadcasted_iota(jnp.int32, (2 * NT * CAP, 256), 1) // 128
    slot_of = ((spot // 32) * 16 + spot % 16).astype(F32)
    put_both[...] = jnp.where((slot_of == wanted) & (side == (spot // 16) % 2), 1.0, 0.0).astype(BF16)

    for order, part in enumerate((x, codes_ring.left, codes_ring.right, codes_ring.far)):
        s_links.wait(z_take.at[pl.ds(pl.multiple_of(part * CROWS, CROWS), CROWS), :], order)

    def own_chunk(chip):
        at = pl.ds(pl.multiple_of(chunk_of(chip, y) * DCH, DCH), DCH)
        return z_own[at, :] + z_take[at, :].astype(F32)

    streams = (
        (8, NZ - 2, (2, 2, 2, 2)),
        (7, NZ - 2, (2, 2, 2, 1)),
        (NZ - 7, 2, (NZ - 2, NZ - 2, NZ - 2, NZ - 1)),
        (NZ - 6, 2, (NZ - 2, NZ - 2, NZ - 2)),
    )

    def ring_copy(number, step):
        return pltpu.make_async_remote_copy(
            src_ref=z_send.at[number, step],
            dst_ref=z_recv.at[number, step],
            send_sem=z_ss.at[number * 4 + step],
            recv_sem=z_rs.at[number * 4 + step],
            device_id={"tok": t, "col": 2 * ((z + streams[number][2][step]) % NZ) + h},
            device_id_type=MESH,
        )

    def ring_step(step):
        for number, (first, change, hops) in enumerate(streams):
            if step < len(hops):
                value = own_chunk((z + first + step * change) % NZ)
                if step > 0:
                    ring_copy(number, step - 1).wait_recv()
                    value = value + z_recv[number, step - 1].astype(F32)
                z_send[number, step] = value.astype(BF16)
                ring_copy(number, step).start()

    ring_step(0)

    for step in (1, 3, 2):
        source = (y + 4 - step) % 4
        mine = x_buf.at[pl.ds(source * ROWS + 64 * h, 64), :]
        x_links.wait(mine, step - 1)
        x_links.start(mine, mine, 3 + step - 1, t, sibling)
    q_ring.forward()
    ring_step(1)

    for step in (1, 3, 2):
        source = (y + 4 - step) % 4
        x_links.wait(x_buf.at[pl.ds(source * ROWS + 64 * (1 - h), 64), :], 3 + step - 1)

    def up_rows(i, carry):
        at = pl.ds(pl.multiple_of(i * ROWS, ROWS), ROWS)
        h_part[at, :] = dot_nn(x_buf[at, :], w_eff[...]).astype(BF16)
        return carry

    lax.fori_loop(0, 4, up_rows, 0)
    h_ring = RingReduce(
        Links(h_ss, h_rs), y, at_y, lambda i: h_part.at[pl.ds(i * ROWS, ROWS), :], rows_half(64),
        h_first, h_stage, h_second,
    )
    h_ring.begin()
    q_ring.finish()
    r_part[...] = q_ring.total(q_part[pl.ds(x * 64, 64), :].astype(F32)).astype(BF16)
    r_ring = RingReduce(
        Links(r_ss, r_rs), y, at_y, lambda i: r_part.at[pl.ds(i * 16, 16), :], lanes_half(512),
        r_first, r_stage, r_second,
    )
    r_ring.begin()
    ring_step(2)
    h_ring.forward()
    r_ring.forward()
    ring_step(3)
    h_ring.finish()
    up_value = h_ring.total(h_part[pl.ds(y * ROWS, ROWS), :].astype(F32)) * row_weight
    hs_send[...] = dot_nn(put_slots, up_value.astype(BF16)).astype(BF16)

    def h_step(i, carry):
        a2a_copy(hs_send, hs_buf, 1, (t + i) % NT).start()
        return carry

    lax.fori_loop(1, NT, h_step, 0)
    hs_buf[own_cap, :] = hs_send[own_cap, :]
    r_ring.finish()
    gradient = r_ring.total(r_part[pl.ds(pl.multiple_of(y * 16, 16), 16), :].astype(F32))

    tops = []
    for j in range(2):
        for k in range(2):
            q = 2 * j + k
            g = gradient[:, q * BLK : (q + 1) * BLK]
            new_m = beta_first * adam_m[:, j, k, :] + (1.0 - beta_first) * g
            new_v = beta_second * adam_v[:, j, k, :] + (1.0 - beta_second) * g * g
            corrected_m = new_m / (1.0 - beta_first**STEP)
            corrected_v = new_v / (1.0 - beta_second**STEP)
            new_delta = delta[:, j, k, :] - step_rate * corrected_m / (
                jnp.sqrt(corrected_v) + adam_eps
            )
            nm_out[:, j, k, :] = new_m
            nv_out[:, j, k, :] = new_v
            nd_out[:, j, k, :] = new_delta
            tops.append(jnp.max(jnp.abs(new_delta)))
    tile_row = lax.broadcasted_iota(jnp.int32, (8, 128), 0)
    tile = jnp.zeros((8, 128), F32)
    for q in range(4):
        tile = jnp.where(tile_row == q, tops[q], tile)
    m_send[...] = tile
    m_buf[t] = tile

    def m_copy(other):
        return pltpu.make_async_remote_copy(
            src_ref=m_send,
            dst_ref=m_buf.at[t],
            send_sem=a_ss.at[2],
            recv_sem=a_rs.at[2],
            device_id={"tok": other, "col": c},
            device_id_type=MESH,
        )

    def m_step(i, carry):
        m_copy((t + i) % NT).start()
        return carry

    lax.fori_loop(1, NT, m_step, 0)

    total = own_chunk(z)
    for number, (first, change, hops) in enumerate(streams):
        ring_copy(number, len(hops) - 1).wait_recv()
        total = total + z_recv[number, len(hops) - 1].astype(F32)
    chunk = jnp.concatenate([total.astype(BF16), jnp.zeros((128 - DCH, 256), BF16)], axis=0)
    f_send[...] = dot_nt(put_both[...], chunk).astype(BF16)

    def f_copy(other):
        return pltpu.make_async_remote_copy(
            src_ref=f_send.at[pl.ds(pl.multiple_of(other * 32, 32), 32), :],
            dst_ref=f_buf.at[pl.ds(pl.multiple_of(t * 32, 32), 32), :],
            send_sem=a_ss.at[3],
            recv_sem=a_rs.at[3],
            device_id={"tok": other, "col": c},
            device_id_type=MESH,
        )

    def f_step(i, carry):
        f_copy((t + i) % NT).start()
        return carry

    lax.fori_loop(1, NT, f_step, 0)
    own_f = pl.ds(pl.multiple_of(t * 32, 32), 32)
    f_buf[own_f, :] = f_send[own_f, :]

    pltpu.make_async_copy(
        hs_buf.at[pl.ds(0, 15 * CAP), :], hs_buf.at[pl.ds(0, 15 * CAP), :], a_rs.at[1]
    ).wait()
    gg_out[...] = (slope[...] * hs_buf[...].astype(F32)).astype(BF16)

    pltpu.make_async_copy(
        f_buf.at[pl.ds(0, 480), :], f_buf.at[pl.ds(0, 480), :], a_rs.at[3]
    ).wait()

    def e_copy(number):
        chunk_here = chunk_of(z, number)
        return pltpu.make_async_remote_copy(
            src_ref=e_send.at[number],
            dst_ref=e_buf.at[pl.ds((chunk_here % 2) * DCH, DCH), pl.ds(pl.multiple_of(h * 128, 128), 128)],
            send_sem=e_ss.at[number],
            recv_sem=e_rs.at[(chunk_here % 2) * 2 + h],
            device_id={"tok": t, "col": end_of(number)},
            device_id_type=MESH,
        )

    some_rows = jnp.where(
        lax.broadcasted_iota(jnp.int32, (DCH, 128), 0) == lax.broadcasted_iota(jnp.int32, (DCH, 128), 1), 1.0, 0.0
    ).astype(BF16)
    for number in range(4):
        held = f_buf[128 * number : 128 * number + 128, :]
        ordered = jnp.concatenate(
            [held[32 * xx + 16 * part : 32 * xx + 16 * part + 16] for part in range(2) for xx in range(4)],
            axis=0,
        )
        e_send[number] = dot_nt(some_rows, ordered).astype(BF16)
        away = end_of(number) != c

        @pl.when(away)
        def _():
            e_copy(number).start()

        @pl.when(jnp.logical_not(away))
        def _():
            e_buf[
                pl.ds(pl.multiple_of((chunk_of(z, number) % 2) * DCH, DCH), DCH),
                pl.ds(pl.multiple_of(h * 128, 128), 128),
            ] = e_send[number]

    pltpu.make_async_copy(m_buf.at[pl.ds(0, 15)], m_buf.at[pl.ds(0, 15)], a_rs.at[2]).wait()
    top = jnp.max(m_buf[...], axis=0)
    for j in range(2):
        for k in range(2):
            q = 2 * j + k
            scale = jnp.max(top[q : q + 1, :])
            ds_out[j, k] = scale
            dc_out[:, j, k, :] = (nd_out[:, j, k, :] / (scale + scale_eps)).astype(BF16)

    for number in range(4):
        other = start_of(number)

        @pl.when(other != c)
        def _():
            block = e_buf.at[
                pl.ds((number // 2) * DCH, DCH), pl.ds((number % 2) * 128, 128)
            ]
            pltpu.make_async_copy(block, block, e_rs.at[number]).wait()

    ig_out[...] = e_buf[...]

    for links in (
        codes_ring.links, x_links, dy_ring.links, dx_ring.links, g_ring.links,
        q_ring.links, r_ring.links, h_ring.links, s_links,
    ):
        links.drain()
    for number, (first, change, hops) in enumerate(streams):
        for step in range(len(hops)):
            ring_copy(number, step).wait_send()
    for number in range(2):
        pltpu.make_async_copy(
            u_buf.at[pl.ds(0, 15 * CAP), :], u_buf.at[pl.ds(0, 15 * CAP), :], a_ss.at[number]
        ).wait()
    pltpu.make_async_copy(m_buf.at[pl.ds(0, 15)], m_buf.at[pl.ds(0, 15)], a_ss.at[2]).wait()
    pltpu.make_async_copy(
        f_buf.at[pl.ds(0, 480), :], f_buf.at[pl.ds(0, 480), :], a_ss.at[3]
    ).wait()
    for number in range(4):

        @pl.when(end_of(number) != c)
        def _():
            e_copy(number).wait_send()


def per_device(
    rollout, lengths, route, up_codes, up_scales, block_rows, delta, adam_m, adam_v, gate_pre, hidden_grad
):
    vmem = pl.BlockSpec(memory_space=pltpu.VMEM)
    smem = pl.BlockSpec(memory_space=pltpu.SMEM)
    dma = pltpu.SemaphoreType.DMA

    def bf(*shape):
        return pltpu.VMEM(shape, BF16)

    def fl(*shape):
        return pltpu.VMEM(shape, F32)

    smem_of = pltpu.SMEM
    block4 = delta.shape
    scratch = [
        smem_of((2,), jnp.int32), smem_of((2, 20), F32), smem_of((2, 2), jnp.int32),
        bf(ROWS, D), pltpu.VMEM((1, ROWS), jnp.int32), fl(*block4), fl(*block4), fl(*block4),
        bf(256, COLS), bf(256, COLS),
        bf(256, COLS), bf(256, COLS), fl(256, COLS), bf(KS, COLS), bf(KS, COLS), bf(4 * ROWS, KS),
        bf(256, 1024), bf(4, GB, COLS), bf(4 * ROWS, COLS),
        bf(4 * ROWS, COLS), bf(2, 64, COLS), bf(2, 64, COLS), bf(2, ROWS, COLS),
        bf(256, COLS), bf(256, COLS),
        bf(256, 1024), bf(2, 32, 1024), bf(2, 32, 1024), bf(2, 64, 1024),
        bf(64, 1024), bf(2, 16, 512), bf(2, 16, 512), bf(2, 16, 1024),
        fl(8, 128), fl(NT, 8, 128), fl(KS, 256), bf(KS, 256), bf(KS, 256),
        bf(4, 4, DCH, 256), bf(4, 4, DCH, 256), bf(512, 128), bf(512, 128), bf(4, DCH, 128), bf(160, 256),
        bf(4, ROWS, BLK), bf(512, 256),
        dma((11,)),
        dma((6,)), dma((6,)), dma((6,)), dma((6,)), dma((6,)), dma((6,)), dma((6,)), dma((6,)),
        dma((6,)), dma((6,)), dma((6,)), dma((6,)), dma((6,)), dma((6,)), dma((6,)), dma((6,)),
        dma((4,)), dma((4,)), dma((16,)), dma((16,)), dma((4,)), dma((4,)), dma((4,)), dma((4,)),
    ]
    block = jax.ShapeDtypeStruct(delta.shape, F32)
    outs = pl.pallas_call(
        kernel,
        out_shape=(
            jax.ShapeDtypeStruct((160, 256), BF16),
            jax.ShapeDtypeStruct((256, COLS), BF16),
            block,
            block,
            block,
            jax.ShapeDtypeStruct((2, 2), F32),
            jax.ShapeDtypeStruct(delta.shape, BF16),
        ),
        in_specs=[pl.BlockSpec(memory_space=pl.ANY)] * 11,
        out_specs=(vmem, vmem, vmem, vmem, vmem, smem, vmem),
        scratch_shapes=scratch,
        compiler_params=pltpu.CompilerParams(
            collective_id=0, has_side_effects=True, vmem_limit_bytes=VLIM * 1024 * 1024
        ),
        cost_estimate=pl.CostEstimate(flops=3 * 10**9, bytes_accessed=4 * 10**6, transcendentals=0),
    )(
        lengths, up_scales.T, block_rows, rollout, route.T, up_codes, delta, adam_m, adam_v, gate_pre, hidden_grad
    )
    return (outs[0].T,) + tuple(outs[1:])


def solution(mesh):
    placed = (
        P("tok", None),
        P("tok"),
        P("tok", None),
        P("tok", "col"),
        P(None, "col"),
        P("col", None),
        P("tok", "col", None, None),
        P("tok", "col", None, None),
        P("tok", "col", None, None),
        P("tok", "col"),
        P("tok", "col"),
    )
    return jax.shard_map(
        per_device,
        mesh=mesh,
        in_specs=placed,
        out_specs=(
            P("tok", "col"),
            P("tok", "col"),
            P("tok", "col", None, None),
            P("tok", "col", None, None),
            P("tok", "col", None, None),
            P("col", None),
            P("tok", "col", None, None),
        ),
        check_vma=False,
    )
```

time: 121 us -> 87.7 us (0.72)
  Pallas kernels: 106 us -> 76.4 us
  local copies, waits for them, and re-layouts: 14.1 us -> 10.2 us
    pallas_call x1, Pallas kernels: 106 us -> 76.4 us  [per_device(): pl.pallas_call(kernel, out_shape=(jax.ShapeDtypeStruct((160, 256), BF16),...]
    unnamed x26 -> x7, local copies, waits for them, and re-layouts: 13.3 us -> 10.2 us
where the time goes in v2:
time: 87.7 us; the launch traced here: 87.3 us
  Pallas kernels  76.4 us (87%)
  local copies, waits for them, and re-layouts  10.2 us (12%)
    pallas_call x1, Pallas kernels, per_device(): pl.pallas_call(kernel, out_shape=(jax.ShapeDtypeStruct((160, 256), BF16),...  76.4 us
    unnamed x7, local copies, waits for them, and re-layouts  10.2 us

profile of v2, /device:TPU:1, one launch (start us, length us, event | category | flops | bytes accessed | tf_op | source)
XLA Modules:
  0.0 87.3 jit_solution(5461992364234819798)
XLA Ops:
  0.6 76.4 %shard_map.162 = (bf16[160,256]{1,0:T(8,128)(2,1)}, bf16[256,512]{1,0:T(8,128)(2,1)}, f32[16,2,2,256]{3,2,1,0:T(2,128)}, f32[16,2,2,256]{3,2,1,0:T(2,128)}, f32[...) custom-call(s32[2]{0:T(128)} %lengths_h.1, f32[2,20]{1,0:T(2,128)} %bitcast.4, ...), custom_call_target="tpu_custom_call" | custom-call | flops 3000000000 | bytes 4000000 | tf_op jit(solution)/shard_map/pallas_call | solution.py:679
  77.1 1.5 %copy.25 = bf16[256,160]{0,1:T(8,128)(2,1)} copy(bf16[256,160]{0,1:T(8,128)(2,1)} %bitcast.3) | data formatting | bytes 163840
  78.6 1.7 %copy.26 = bf16[256,512]{1,0:T(8,128)(2,1)} copy(bf16[256,512]{1,0:T(8,128)(2,1)} %get-tuple-element.29) | data formatting | bytes 524288
  80.3 1.5 %copy.27 = f32[16,2,2,256]{3,2,1,0:T(2,128)} copy(f32[16,2,2,256]{3,2,1,0:T(2,128)} %get-tuple-element.30) | data formatting | bytes 131072
  81.7 1.5 %copy.28 = f32[16,2,2,256]{3,2,1,0:T(2,128)} copy(f32[16,2,2,256]{3,2,1,0:T(2,128)} %get-tuple-element.31) | data formatting | bytes 131072
  83.2 1.5 %copy.29 = f32[16,2,2,256]{3,2,1,0:T(2,128)} copy(f32[16,2,2,256]{3,2,1,0:T(2,128)} %get-tuple-element.32) | data formatting | bytes 131072
  84.7 1.2 %copy.30 = f32[2,2]{1,0:T(2,128)} copy(f32[2,2]{1,0:T(2,128)} %get-tuple-element.33) | data formatting | bytes 32
  85.9 1.4 %copy.31 = bf16[16,2,2,256]{3,2,1,0:T(2,128)(2,1)} copy(bf16[16,2,2,256]{3,2,1,0:T(2,128)(2,1)} %get-tuple-element.34) | data formatting | bytes 65536

commit v3 on v2

--- a/solution.py
+++ b/solution.py
@@ -9,6 +9,7 @@
 
 BLK = 256
 VLIM = 62
+VLIM2 = 62
 RESP = 64
 STEP = 1000
 D = 5120
@@ -106,6 +107,20 @@
         self.got(self.right, 0, 3)
         self.got(self.far, 0, 4)
         self.got(self.far, 1, 5)
+
+
+class DirectGather:
+    def __init__(self, links, me, device, block):
+        self.links, self.me, self.device, self.block = links, me, device, block
+
+    def begin(self):
+        for step in (1, 3, 2):
+            own = self.block(self.me)
+            self.links.start(own, own, step - 1, *self.device((self.me + step) % 4))
+
+    def finish(self):
+        for step in (1, 3, 2):
+            self.links.wait(self.block((self.me + 4 - step) % 4), step - 1)
 
 
 class RingReduce:
@@ -245,10 +260,10 @@
 
     lax.fori_loop(0, 8, gate_rows, 0)
 
-    dy_ring = RingGather(
-        Links(dy_ss, dy_rs), y, at_y, lambda i: d_buf.at[pl.ds(x * 64 + i * 16, 16), :], lanes_half(512)
-    )
-    own_delta = dy_ring.block(y)
+    dx_ring = DirectGather(
+        Links(dx_ss, dx_rs), x, at_x, lambda i: d_buf.at[pl.ds(y * 64 + i * 16, 16), :]
+    )
+    own_delta = dx_ring.block(x)
     loads[2].wait()
     for j in range(2):
         for k in range(2):
@@ -256,6 +271,8 @@
     loads[3].wait()
 
     pl.semaphore_wait(barrier, jnp.where(stays, 26, 28))
+
+    dx_ring.begin()
 
     def a2a_copy(src, dst, number, other):
         return pltpu.make_async_remote_copy(
@@ -274,7 +291,6 @@
     lax.fori_loop(1, NT, u_step, 0)
     own_cap = pl.ds(pl.multiple_of(t * CAP, CAP), CAP)
     u_buf[own_cap, :] = u_send[own_cap, :]
-    dy_ring.begin(own_delta)
 
     codes_ring = RingGather(
         Links(c_ss, c_rs), x, at_x, lambda i: w_buf.at[pl.ds(i * CROWS, CROWS), :], rows_half(CROWS // 2)
@@ -302,6 +318,12 @@
     live = jnp.where(row_id < RESP, lengths[0], lengths[1])
     row_weight = jnp.where(row_id % RESP < live, RESP / live.astype(F32), 0.0)
 
+    dx_ring.finish()
+    dy_ring = RingGather(
+        Links(dy_ss, dy_rs), y, at_y, lambda i: d_buf.at[pl.ds(i * 64, 64), :], rows_half(32)
+    )
+    dy_ring.begin(dy_ring.block(y))
+
     pltpu.make_async_copy(
         u_buf.at[pl.ds(0, 15 * CAP), :], u_buf.at[pl.ds(0, 15 * CAP), :], a_rs.at[0]
     ).wait()
@@ -312,13 +334,8 @@
     own_g[ROWS:GB, :] = jnp.concatenate([target_row[0 : GB - ROWS, :]] * 4, axis=1).astype(BF16)
     g_ring.begin(own_g)
 
+    codes_ring.forward()
     dy_ring.forward()
-    codes_ring.forward()
-    dy_ring.finish()
-    dx_ring = RingGather(
-        Links(dx_ss, dx_rs), x, at_x, lambda i: d_buf.at[pl.ds(i * 64, 64), :], rows_half(32)
-    )
-    dx_ring.begin(dx_ring.block(x))
     g_ring.forward()
 
     x_links = Links(x_ss, x_rs)
@@ -361,8 +378,7 @@
     q_ring.begin()
     x_buf[pl.ds(y * ROWS, ROWS), :] = rollout[:, pl.ds(pl.multiple_of(y * KS, KS), KS)]
 
-    dx_ring.forward()
-    dx_ring.finish()
+    dy_ring.finish()
     g_ring.finish()
     for yy in range(4):
         g_all[ROWS * yy : ROWS * (yy + 1), :] = g_buf[yy, 0:ROWS, :]
@@ -373,14 +389,13 @@
         for j in range(2):
             scale = scales[j, block]
             on = [is_same(brows[j, k], block) for k in range(2)]
-            for xx in range(4):
-                at = pl.ds(pl.multiple_of(index * 64 + xx * 16, 16), 16)
-                held = pl.ds(pl.multiple_of(64 * xx + 16 * part, 16), 16)
-                value = w_buf[at, j * BLK : (j + 1) * BLK].astype(F32) * scale
-                for k in range(2):
-                    q = 2 * j + k
-                    value = value + on[k] * d_buf[held, q * BLK : (q + 1) * BLK].astype(F32)
-                w_eff[at, j * BLK : (j + 1) * BLK] = value.astype(BF16)
+            at = pl.ds(pl.multiple_of(index * 64, 64), 64)
+            held = pl.ds(pl.multiple_of(64 * part, 64), 64)
+            value = w_buf[at, j * BLK : (j + 1) * BLK].astype(F32) * scale
+            for k in range(2):
+                q = 2 * j + k
+                value = value + on[k] * d_buf[held, q * BLK : (q + 1) * BLK].astype(F32)
+            w_eff[at, j * BLK : (j + 1) * BLK] = value.astype(BF16)
         return carry
 
     s_links = Links(s_ss, s_rs)
@@ -415,12 +430,7 @@
         at = pl.ds(pl.multiple_of(chunk_of(chip, y) * DCH, DCH), DCH)
         return z_own[at, :] + z_take[at, :].astype(F32)
 
-    streams = (
-        (8, NZ - 2, (2, 2, 2, 2)),
-        (7, NZ - 2, (2, 2, 2, 1)),
-        (NZ - 7, 2, (NZ - 2, NZ - 2, NZ - 2, NZ - 1)),
-        (NZ - 6, 2, (NZ - 2, NZ - 2, NZ - 2)),
-    )
+    streams = ((2, 8, NZ - 2, 4), (NZ - 2, NZ - 6, 2, 3), (1, 7, NZ - 2, 4), (NZ - 1, NZ - 7, 2, 4))
 
     def ring_copy(number, step):
         return pltpu.make_async_remote_copy(
@@ -428,45 +438,42 @@
             dst_ref=z_recv.at[number, step],
             send_sem=z_ss.at[number * 4 + step],
             recv_sem=z_rs.at[number * 4 + step],
-            device_id={"tok": t, "col": 2 * ((z + streams[number][2][step]) % NZ) + h},
+            device_id={"tok": t, "col": 2 * ((z + streams[number][0]) % NZ) + h},
             device_id_type=MESH,
         )
 
+    def ring_send(number, step, *joins):
+        hops, first, change, steps = streams[number]
+        value = own_chunk((z + first + step * change) % NZ)
+        for stream, index in joins:
+            ring_copy(stream, index).wait_recv()
+            value = value + z_recv[stream, index].astype(F32)
+        z_send[number, step] = value.astype(BF16)
+        ring_copy(number, step).start()
+
     def ring_step(step):
-        for number, (first, change, hops) in enumerate(streams):
-            if step < len(hops):
-                value = own_chunk((z + first + step * change) % NZ)
-                if step > 0:
-                    ring_copy(number, step - 1).wait_recv()
-                    value = value + z_recv[number, step - 1].astype(F32)
-                z_send[number, step] = value.astype(BF16)
-                ring_copy(number, step).start()
+        if step == 0:
+            ring_send(0, 0)
+            ring_send(3, 0)
+            ring_send(2, 0)
+            ring_send(3, 1)
+            ring_send(2, 1)
+            ring_send(1, 0, (3, 0))
+        else:
+            ring_send(0, step, (2, step - 1), (0, step - 1))
+            if step < 3:
+                ring_send(1, step, (3, step), (1, step - 1))
+                ring_send(3, step + 1)
+                ring_send(2, step + 1)
 
     ring_step(0)
-
+    q_ring.forward()
     for step in (1, 3, 2):
         source = (y + 4 - step) % 4
         mine = x_buf.at[pl.ds(source * ROWS + 64 * h, 64), :]
         x_links.wait(mine, step - 1)
         x_links.start(mine, mine, 3 + step - 1, t, sibling)
-    q_ring.forward()
     ring_step(1)
-
-    for step in (1, 3, 2):
-        source = (y + 4 - step) % 4
-        x_links.wait(x_buf.at[pl.ds(source * ROWS + 64 * (1 - h), 64), :], 3 + step - 1)
-
-    def up_rows(i, carry):
-        at = pl.ds(pl.multiple_of(i * ROWS, ROWS), ROWS)
-        h_part[at, :] = dot_nn(x_buf[at, :], w_eff[...]).astype(BF16)
-        return carry
-
-    lax.fori_loop(0, 4, up_rows, 0)
-    h_ring = RingReduce(
-        Links(h_ss, h_rs), y, at_y, lambda i: h_part.at[pl.ds(i * ROWS, ROWS), :], rows_half(64),
-        h_first, h_stage, h_second,
-    )
-    h_ring.begin()
     q_ring.finish()
     r_part[...] = q_ring.total(q_part[pl.ds(x * 64, 64), :].astype(F32)).astype(BF16)
     r_ring = RingReduce(
@@ -475,19 +482,24 @@
     )
     r_ring.begin()
     ring_step(2)
-    h_ring.forward()
+
+    for step in (1, 3, 2):
+        source = (y + 4 - step) % 4
+        x_links.wait(x_buf.at[pl.ds(source * ROWS + 64 * (1 - h), 64), :], 3 + step - 1)
+
+    def up_rows(i, carry):
+        at = pl.ds(pl.multiple_of(i * ROWS, ROWS), ROWS)
+        h_part[at, :] = dot_nn(x_buf[at, :], w_eff[...]).astype(BF16)
+        return carry
+
+    lax.fori_loop(0, 4, up_rows, 0)
+    h_ring = RingReduce(
+        Links(h_ss, h_rs), y, at_y, lambda i: h_part.at[pl.ds(i * ROWS, ROWS), :], rows_half(64),
+        h_first, h_stage, h_second,
+    )
+    h_ring.begin()
     r_ring.forward()
     ring_step(3)
-    h_ring.finish()
-    up_value = h_ring.total(h_part[pl.ds(y * ROWS, ROWS), :].astype(F32)) * row_weight
-    hs_send[...] = dot_nn(put_slots, up_value.astype(BF16)).astype(BF16)
-
-    def h_step(i, carry):
-        a2a_copy(hs_send, hs_buf, 1, (t + i) % NT).start()
-        return carry
-
-    lax.fori_loop(1, NT, h_step, 0)
-    hs_buf[own_cap, :] = hs_send[own_cap, :]
     r_ring.finish()
     gradient = r_ring.total(r_part[pl.ds(pl.multiple_of(y * 16, 16), 16), :].astype(F32))
 
@@ -531,9 +543,9 @@
     lax.fori_loop(1, NT, m_step, 0)
 
     total = own_chunk(z)
-    for number, (first, change, hops) in enumerate(streams):
-        ring_copy(number, len(hops) - 1).wait_recv()
-        total = total + z_recv[number, len(hops) - 1].astype(F32)
+    for number, (hops, first, change, steps) in enumerate(streams):
+        ring_copy(number, steps - 1).wait_recv()
+        total = total + z_recv[number, steps - 1].astype(F32)
     chunk = jnp.concatenate([total.astype(BF16), jnp.zeros((128 - DCH, 256), BF16)], axis=0)
     f_send[...] = dot_nt(put_both[...], chunk).astype(BF16)
 
@@ -555,10 +567,17 @@
     own_f = pl.ds(pl.multiple_of(t * 32, 32), 32)
     f_buf[own_f, :] = f_send[own_f, :]
 
-    pltpu.make_async_copy(
-        hs_buf.at[pl.ds(0, 15 * CAP), :], hs_buf.at[pl.ds(0, 15 * CAP), :], a_rs.at[1]
-    ).wait()
-    gg_out[...] = (slope[...] * hs_buf[...].astype(F32)).astype(BF16)
+    h_ring.forward()
+    h_ring.finish()
+    up_value = h_ring.total(h_part[pl.ds(y * ROWS, ROWS), :].astype(F32)) * row_weight
+    hs_send[...] = dot_nn(put_slots, up_value.astype(BF16)).astype(BF16)
+
+    def h_step(i, carry):
+        a2a_copy(hs_send, hs_buf, 1, (t + i) % NT).start()
+        return carry
+
+    lax.fori_loop(1, NT, h_step, 0)
+    hs_buf[own_cap, :] = hs_send[own_cap, :]
 
     pltpu.make_async_copy(
         f_buf.at[pl.ds(0, 480), :], f_buf.at[pl.ds(0, 480), :], a_rs.at[3]
@@ -607,6 +626,11 @@
             ds_out[j, k] = scale
             dc_out[:, j, k, :] = (nd_out[:, j, k, :] / (scale + scale_eps)).astype(BF16)
 
+    pltpu.make_async_copy(
+        hs_buf.at[pl.ds(0, 15 * CAP), :], hs_buf.at[pl.ds(0, 15 * CAP), :], a_rs.at[1]
+    ).wait()
+    gg_out[...] = (slope[...] * hs_buf[...].astype(F32)).astype(BF16)
+
     for number in range(4):
         other = start_of(number)
 
@@ -624,8 +648,8 @@
         q_ring.links, r_ring.links, h_ring.links, s_links,
     ):
         links.drain()
-    for number, (first, change, hops) in enumerate(streams):
-        for step in range(len(hops)):
+    for number, (hops, first, change, steps) in enumerate(streams):
+        for step in range(steps):
             ring_copy(number, step).wait_send()
     for number in range(2):
         pltpu.make_async_copy(
@@ -640,6 +664,14 @@
         @pl.when(end_of(number) != c)
         def _():
             e_copy(number).wait_send()
+
+
+def settle(*refs):
+    for held, out in zip(refs[:6], refs[7:13]):
+        out[...] = held[...]
+    for j in range(2):
+        for k in range(2):
+            refs[13][j, k] = refs[6][j, k]
 
 
 def per_device(
@@ -697,7 +729,16 @@
     )(
         lengths, up_scales.T, block_rows, rollout, route.T, up_codes, delta, adam_m, adam_v, gate_pre, hidden_grad
     )
-    return (outs[0].T,) + tuple(outs[1:])
+    large = outs[:5] + outs[6:]
+    shapes = tuple(jax.ShapeDtypeStruct(held.shape, held.dtype) for held in large)
+    results = pl.pallas_call(
+        settle,
+        out_shape=shapes + (jax.ShapeDtypeStruct((2, 2), F32),),
+        in_specs=[vmem] * 6 + [smem],
+        out_specs=(vmem,) * 6 + (smem,),
+        compiler_params=pltpu.CompilerParams(vmem_limit_bytes=VLIM2 * 1024 * 1024),
+    )(*large, outs[5])
+    return (results[0].T,) + tuple(results[1:5]) + (results[6], results[5])
 
 
 def solution(mesh):

time: 87.7 us -> 74.1 us (0.84)
  local copies, waits for them, and re-layouts: 10.2 us -> 0 us
  Pallas kernels: 76.4 us -> 73.3 us
    unnamed x7 -> x0, local copies, waits for them, and re-layouts: 10.2 us -> none
    pallas_call x1, Pallas kernels: 76.4 us -> 71.4 us  [per_device(): pl.pallas_call(kernel, out_shape=(jax.ShapeDtypeStruct((160, 256), BF16),...]
    pallas_call x0 -> x1, Pallas kernels: none -> 1.86 us  [per_device(): pl.pallas_call(settle, out_shape=shapes + (jax.ShapeDtypeStruct((2, 2), F...]
where the time goes in v3:
time: 74.1 us; the launch traced here: 73.9 us
  Pallas kernels  73.3 us (99%)
    pallas_call x1, Pallas kernels, per_device(): pl.pallas_call(kernel, out_shape=(jax.ShapeDtypeStruct((160, 256), BF16),...  71.4 us
    pallas_call x1, Pallas kernels, per_device(): pl.pallas_call(settle, out_shape=shapes + (jax.ShapeDtypeStruct((2, 2), F...  1.86 us

profile of v3, /device:TPU:1, one launch (start us, length us, event | category | flops | bytes accessed | tf_op | source)
XLA Modules:
  0.0 73.9 jit_solution(9431283116445943998)
XLA Ops:
  0.6 71.4 %shard_map.162 = (bf16[160,256]{1,0:T(8,128)(2,1)}, bf16[256,512]{1,0:T(8,128)(2,1)}, f32[16,2,2,256]{3,2,1,0:T(2,128)}, f32[16,2,2,256]{3,2,1,0:T(2,128)}, f32[...) custom-call(s32[2]{0:T(128)} %lengths_h.1, f32[2,20]{1,0:T(2,128)} %bitcast.4, ...), custom_call_target="tpu_custom_call" | custom-call | flops 3000000000 | bytes 4000000 | tf_op jit(solution)/shard_map/pallas_call | solution.py:711
  72.0 1.9 %shard_map.163 = (bf16[160,256]{1,0:T(8,128)(2,1)}, bf16[256,512]{1,0:T(8,128)(2,1)}, f32[16,2,2,256]{3,2,1,0:T(2,128)}, f32[16,2,2,256]{3,2,1,0:T(2,128)}, f32[...) custom-call(bf16[160,256]{1,0:T(8,128)(2,1)} %get-tuple-element.21.refs_0_, ...), custom_call_target="tpu_custom_call" | custom-call | tf_op jit(solution)/shard_map/pallas_call | solution.py:734

commit v4 on v3

--- a/solution.py
+++ b/solution.py
@@ -91,8 +91,14 @@
         self.links.wait(self.half(self.block(index), part), number)
 
     def begin(self, src):
+        self.begin_far(src)
+        self.begin_near(src)
+
+    def begin_far(self, src):
         self.put(src, self.me, 0, 0, self.right)
         self.put(src, self.me, 1, 1, self.left)
+
+    def begin_near(self, src):
         self.put(src, self.me, 1, 2, self.right)
         self.put(src, self.me, 0, 3, self.left)
 
@@ -209,7 +215,7 @@
         (scales_h, scales), (m_h, adam_m), (v_h, adam_v),
     )
     loads = [pltpu.make_async_copy(src, dst, in_s.at[i]) for i, (src, dst) in enumerate(pairs)]
-    for load in loads:
+    for load in loads[:4]:
         load.start()
 
     def chunk_of(chip, row):
@@ -244,6 +250,8 @@
             def _():
                 greet(t, other)
 
+    for load in loads[4:]:
+        load.start()
     stays = end_of(z // 4) == c
 
     loads[0].wait()
@@ -295,7 +303,7 @@
     codes_ring = RingGather(
         Links(c_ss, c_rs), x, at_x, lambda i: w_buf.at[pl.ds(i * CROWS, CROWS), :], rows_half(CROWS // 2)
     )
-    codes_ring.begin(own_codes)
+    codes_ring.begin_far(own_codes)
 
     for load in loads[4:]:
         load.wait()
@@ -333,20 +341,11 @@
     own_g[0:ROWS, :] = up_grad
     own_g[ROWS:GB, :] = jnp.concatenate([target_row[0 : GB - ROWS, :]] * 4, axis=1).astype(BF16)
     g_ring.begin(own_g)
+    codes_ring.begin_near(own_codes)
 
     codes_ring.forward()
     dy_ring.forward()
     g_ring.forward()
-
-    x_links = Links(x_ss, x_rs)
-    for step in (1, 3, 2):
-        to = (y + step) % 4
-        x_links.start(
-            rollout.at[pl.ds(64 * h, 64), pl.ds(pl.multiple_of(to * KS, KS), KS)],
-            x_buf.at[pl.ds(y * ROWS + 64 * h, 64), :],
-            step - 1,
-            *at_y(to),
-        )
 
     def choose_rows(i, carry):
         at = pl.ds(pl.multiple_of(i * 32, 32), 32)
@@ -375,13 +374,23 @@
         Links(q_ss, q_rs), x, at_x, lambda i: q_part.at[pl.ds(i * 64, 64), :], rows_half(32),
         q_first, q_stage, q_second,
     )
-    q_ring.begin()
     x_buf[pl.ds(y * ROWS, ROWS), :] = rollout[:, pl.ds(pl.multiple_of(y * KS, KS), KS)]
 
     dy_ring.finish()
     g_ring.finish()
     for yy in range(4):
         g_all[ROWS * yy : ROWS * (yy + 1), :] = g_buf[yy, 0:ROWS, :]
+
+    x_links = Links(x_ss, x_rs)
+    for step in (1, 3, 2):
+        to = (y + step) % 4
+        x_links.start(
+            rollout.at[pl.ds(64 * h, 64), pl.ds(pl.multiple_of(to * KS, KS), KS)],
+            x_buf.at[pl.ds(y * ROWS + 64 * h, 64), :],
+            step - 1,
+            *at_y(to),
+        )
+
 
     def weight_rows(index, carry):
         block = y * 5 + index // 4
@@ -409,6 +418,7 @@
         if order == 3:
             codes_ring.got(part, 0, 4)
             codes_ring.got(part, 1, 5)
+            q_ring.begin()
         lax.fori_loop(5 * part, 5 * part + 5, weight_rows, 0)
         at = pl.ds(pl.multiple_of(part * CROWS, CROWS), CROWS)
         z_give[at, :] = dot_nt(w_eff[at, :], g_all[give_rows, :]).astype(BF16)
@@ -500,6 +510,32 @@
     h_ring.begin()
     r_ring.forward()
     ring_step(3)
+    total = own_chunk(z)
+    for number, (hops, first, change, steps) in enumerate(streams):
+        ring_copy(number, steps - 1).wait_recv()
+        total = total + z_recv[number, steps - 1].astype(F32)
+    chunk = jnp.concatenate([total.astype(BF16), jnp.zeros((128 - DCH, 256), BF16)], axis=0)
+    f_send[...] = dot_nt(put_both[...], chunk).astype(BF16)
+
+    def f_copy(other):
+        return pltpu.make_async_remote_copy(
+            src_ref=f_send.at[pl.ds(pl.multiple_of(other * 32, 32), 32), :],
+            dst_ref=f_buf.at[pl.ds(pl.multiple_of(t * 32, 32), 32), :],
+            send_sem=a_ss.at[3],
+            recv_sem=a_rs.at[3],
+            device_id={"tok": other, "col": c},
+            device_id_type=MESH,
+        )
+
+    def f_step(i, carry):
+        f_copy((t + i) % NT).start()
+        return carry
+
+    lax.fori_loop(1, NT, f_step, 0)
+    own_f = pl.ds(pl.multiple_of(t * 32, 32), 32)
+    f_buf[own_f, :] = f_send[own_f, :]
+
+    h_ring.forward()
     r_ring.finish()
     gradient = r_ring.total(r_part[pl.ds(pl.multiple_of(y * 16, 16), 16), :].astype(F32))
 
@@ -542,32 +578,6 @@
 
     lax.fori_loop(1, NT, m_step, 0)
 
-    total = own_chunk(z)
-    for number, (hops, first, change, steps) in enumerate(streams):
-        ring_copy(number, steps - 1).wait_recv()
-        total = total + z_recv[number, steps - 1].astype(F32)
-    chunk = jnp.concatenate([total.astype(BF16), jnp.zeros((128 - DCH, 256), BF16)], axis=0)
-    f_send[...] = dot_nt(put_both[...], chunk).astype(BF16)
-
-    def f_copy(other):
-        return pltpu.make_async_remote_copy(
-            src_ref=f_send.at[pl.ds(pl.multiple_of(other * 32, 32), 32), :],
-            dst_ref=f_buf.at[pl.ds(pl.multiple_of(t * 32, 32), 32), :],
-            send_sem=a_ss.at[3],
-            recv_sem=a_rs.at[3],
-            device_id={"tok": other, "col": c},
-            device_id_type=MESH,
-        )
-
-    def f_step(i, carry):
-        f_copy((t + i) % NT).start()
-        return carry
-
-    lax.fori_loop(1, NT, f_step, 0)
-    own_f = pl.ds(pl.multiple_of(t * 32, 32), 32)
-    f_buf[own_f, :] = f_send[own_f, :]
-
-    h_ring.forward()
     h_ring.finish()
     up_value = h_ring.total(h_part[pl.ds(y * ROWS, ROWS), :].astype(F32)) * row_weight
     hs_send[...] = dot_nn(put_slots, up_value.astype(BF16)).astype(BF16)

time: 74.1 us -> 72.1 us (0.973); the launches traced: 73.9 us -> 70.9 us
  Pallas kernels: 73.3 us -> 70.3 us
    pallas_call x1, Pallas kernels: 71.4 us -> 68.4 us  [per_device(): pl.pallas_call(kernel, out_shape=(jax.ShapeDtypeStruct((160, 256), BF16),...]
where the time goes in v4:
time: 72.1 us; the launch traced here: 70.9 us
  Pallas kernels  70.3 us (98%)
    pallas_call x1, Pallas kernels, per_device(): pl.pallas_call(kernel, out_shape=(jax.ShapeDtypeStruct((160, 256), BF16),...  68.4 us
    pallas_call x1, Pallas kernels, per_device(): pl.pallas_call(settle, out_shape=shapes + (jax.ShapeDtypeStruct((2, 2), F...  1.86 us

profile of v4, /device:TPU:1, one launch (start us, length us, event | category | flops | bytes accessed | tf_op | source)
XLA Modules:
  0.0 70.9 jit_solution(1040361985286587738)
XLA Ops:
  0.6 68.4 %shard_map.162 = (bf16[160,256]{1,0:T(8,128)(2,1)}, bf16[256,512]{1,0:T(8,128)(2,1)}, f32[16,2,2,256]{3,2,1,0:T(2,128)}, f32[16,2,2,256]{3,2,1,0:T(2,128)}, f32[...) custom-call(s32[2]{0:T(128)} %lengths_h.1, f32[2,20]{1,0:T(2,128)} %bitcast.4, ...), custom_call_target="tpu_custom_call" | custom-call | flops 3000000000 | bytes 4000000 | tf_op jit(solution)/shard_map/pallas_call | solution.py:721
  69.1 1.9 %shard_map.163 = (bf16[160,256]{1,0:T(8,128)(2,1)}, bf16[256,512]{1,0:T(8,128)(2,1)}, f32[16,2,2,256]{3,2,1,0:T(2,128)}, f32[16,2,2,256]{3,2,1,0:T(2,128)}, f32[...) custom-call(bf16[160,256]{1,0:T(8,128)(2,1)} %get-tuple-element.21.refs_0_, ...), custom_call_target="tpu_custom_call" | custom-call | tf_op jit(solution)/shard_map/pallas_call | solution.py:744
